TPU v7x, 32 devices: a whole 2x2x4 slice. The times are simulated.
32 devices in a mesh: dp: 8 (over y, x, core), mp: 4 (over z).
Axes of the slice: x: 2, y: 2, z: 4, core: 2. Of those that a mesh axis runs over, the one named last changes fastest.
Arguments:
- tokens: bfloat16 [3072, 768], P('dp'), may hold values from -6 to 6
- char_ids: int32 [8, 1536], P('dp'), may hold values from 0 to 999
- token_chars: int32 [8, 384], P('dp'), may hold values from 1 to 8, 1536 in all within a row
- groups: int32 [8], P('dp'), may hold values from 0 to 15
- qkv_weight: bfloat16 [768, 3, 768], P('dp', None, 'mp'), may hold values from -0.21875 to 0.21875
- out_weight: bfloat16 [768, 768], P('mp', 'dp'), may hold values from -6 to 6
- ffn_in: bfloat16 [768, 3072], P('dp', 'mp'), may hold values from -0.21875 to 0.21875
- ffn_out: bfloat16 [3072, 768], P('mp', 'dp'), may hold values from -0.109375 to 0.109375
- conv_weight: bfloat16 [4608, 768], P('dp', 'mp'), may hold values from -0.09375 to 0.09375
- gains: bfloat16 [4, 768], P(None, 'dp'), may hold values from 0.5 to 1.5
- ih_weight: bfloat16 [256, 2304], P(('dp', 'mp')), may hold values from -0.375 to 0.375
- hh_weight: bfloat16 [2304, 384], P(('dp', 'mp')), may hold values from -0.3125 to 0.3125
- gru_bias: bfloat16 [2, 1536], P(None, ('dp', 'mp')), may hold values from -3 to 3
- char_table: bfloat16 [1000, 256], P(None, ('dp', 'mp')), may hold values from -6 to 6
- group_table: bfloat16 [16, 256], P(None, ('dp', 'mp')), may hold values from -3 to 3
- token_cot: bfloat16 [3072, 768], P('dp'), may hold values from -6 to 6
- char_cot: bfloat16 [3072, 768], P('dp'), may hold values from -6 to 6
Outputs:
- token_out: bfloat16 [3072, 768], P('dp')
- char_out: bfloat16 [3072, 768], P('dp')
- token_grad: float32 [3072, 768], P('dp')
- qkv_grad: float32 [768, 3, 768], P('dp', None, 'mp')
- out_grad: float32 [768, 768], P('mp', 'dp')
- ffn_in_grad: float32 [768, 3072], P('dp', 'mp')
- ffn_out_grad: float32 [3072, 768], P('mp', 'dp')
- conv_grad: float32 [4608, 768], P('dp', 'mp')
- gain_grad: float32 [4, 768], P(None, 'dp')
- ih_grad: float32 [256, 2304], P(('dp', 'mp'))
- hh_grad: float32 [2304, 384], P(('dp', 'mp'))
- bias_grad: float32 [2, 1536], P(None, ('dp', 'mp'))
- table_grad: float32 [1000, 256], P(None, ('dp', 'mp'))
- group_grad: float32 [16, 256], P(None, ('dp', 'mp'))
Inputs may be any that keep to these rules, and one draw needn't show every extreme that they name: Each row of token_chars sums to 1536 and holds the value 8 somewhere.
All inputs are finite; a program needn't handle non-finite values.
Results may differ from a plain program's by a relative error of at most 0.023.
Values may be sent and summed in bfloat16 or wider, within the bound.
No kernel may reach another device: no remote copies, remote signals or barrier semaphores. Data moves between devices by JAX's collectives and lax.ppermute only.
A program may use at most 192 MiB of HBM per device.

v0:
```python
import jax
import jax.numpy as jnp
from jax import lax
from jax.sharding import PartitionSpec as P

HEADS = 12
MAXC = 8


NORM_EPS = 1e-05


def norm_rows(rows_in, gain_row):
    row_mean = jnp.mean(rows_in, axis=-1, keepdims=True)
    centred = rows_in - row_mean
    spread = jnp.mean(centred * centred, axis=-1, keepdims=True)
    return centred * lax.rsqrt(spread + NORM_EPS) * gain_row


def gelu_fn(rows_in):
    return jax.nn.gelu(rows_in, approximate=True)


def product(left_op, right_op):
    return jnp.dot(left_op, right_op, preferred_element_type=jnp.float32)


def product_tn(left_op, right_op):
    return lax.dot_general(
        left_op, right_op, (((0,), (0,)), ((), ())), preferred_element_type=jnp.float32
    )


def product_nt(left_op, right_op):
    return lax.dot_general(
        left_op, right_op, (((1,), (1,)), ((), ())), preferred_element_type=jnp.float32
    )


def pull_back(function, inputs, cotangent):
    return jax.vjp(function, *inputs)[1](cotangent)


def rows_earlier(rows_in):
    return jnp.concatenate([jnp.zeros_like(rows_in[:1]), rows_in[:-1]], 0)


def rows_later(rows_in):
    return jnp.concatenate([rows_in[1:], jnp.zeros_like(rows_in[:1])], 0)


def attend_forward(query_rows, key_rows, values):
    scores = (
        jnp.einsum("qhd,khd->hqk", query_rows, key_rows, preferred_element_type=jnp.float32) * 0.125
    )
    peak_score = jnp.max(scores, axis=-1, keepdims=True)
    raised = jnp.exp(scores - peak_score)
    row_total = jnp.sum(raised, axis=-1, keepdims=True)
    attn_probs = (raised / row_total).astype(jnp.bfloat16)
    head_out = jnp.einsum("hqk,khd->qhd", attn_probs, values, preferred_element_type=jnp.float32)
    return (head_out, (peak_score + jnp.log(row_total))[..., 0])


def attend_backward(query_rows, key_rows, values, log_sum, grad_out):
    scores = (
        jnp.einsum("qhd,khd->hqk", query_rows, key_rows, preferred_element_type=jnp.float32) * 0.125
    )
    attn_probs = jnp.exp(scores - log_sum[..., None])
    grad_probs = jnp.einsum("qhd,khd->hqk", grad_out, values, preferred_element_type=jnp.float32)
    inner_sum = jnp.sum(grad_probs * attn_probs, axis=-1, keepdims=True)
    grad_scores = (attn_probs * (grad_probs - inner_sum)).astype(jnp.bfloat16)
    query_grad = (
        jnp.einsum("hqk,khd->qhd", grad_scores, key_rows, preferred_element_type=jnp.float32)
        * 0.125
    )
    key_grad = (
        jnp.einsum("hqk,qhd->khd", grad_scores, query_rows, preferred_element_type=jnp.float32)
        * 0.125
    )
    value_grad = jnp.einsum(
        "hqk,qhd->khd",
        attn_probs.astype(jnp.bfloat16),
        grad_out,
        preferred_element_type=jnp.float32,
    )
    return (query_grad, key_grad, value_grad)


def recur_forward(gate_in, rec_weight, bias_row, live_slots):
    unit_count = rec_weight.shape[1]
    hidden_state = jnp.zeros((gate_in.shape[0], unit_count), jnp.float32)
    saved_steps = []
    for position in range(gate_in.shape[1]):
        state_low = hidden_state.astype(jnp.bfloat16)
        recurrent = product_nt(state_low, rec_weight)
        inputs_now = gate_in[:, position]
        reset_gate = jax.nn.sigmoid(
            inputs_now[:, :unit_count] + bias_row[:unit_count] + recurrent[:, :unit_count]
        )
        update = jax.nn.sigmoid(
            inputs_now[:, unit_count : 2 * unit_count]
            + bias_row[unit_count : 2 * unit_count]
            + recurrent[:, unit_count : 2 * unit_count]
        )
        carried = recurrent[:, 2 * unit_count :] + bias_row[3 * unit_count :]
        fresh_state = jnp.tanh(
            inputs_now[:, 2 * unit_count :]
            + bias_row[2 * unit_count : 3 * unit_count]
            + reset_gate * carried
        )
        moved_state = (1.0 - update) * fresh_state + update * hidden_state
        saved_steps.append((hidden_state, state_low, reset_gate, update, carried, fresh_state))
        hidden_state = hidden_state + live_slots[:, position : position + 1] * (
            moved_state - hidden_state
        )
    return (hidden_state, saved_steps)


def recur_backward(grad_state, saved_steps, rec_weight, live_slots):
    unit_count = rec_weight.shape[1]
    gate_grads = []
    weight_grad = jnp.zeros(rec_weight.shape, jnp.float32)
    bias_grad = jnp.zeros((4 * unit_count,), jnp.float32)
    for position in range(len(saved_steps) - 1, -1, -1):
        prev_state, prev_low, reset_gate, update, carried, fresh_state = saved_steps[position]
        grad_moved = live_slots[:, position : position + 1] * grad_state
        grad_prev = grad_state - grad_moved
        grad_fresh = grad_moved * (1.0 - update)
        grad_update = grad_moved * (prev_state - fresh_state)
        grad_prev = grad_prev + grad_moved * update
        grad_inner = grad_fresh * (1.0 - fresh_state * fresh_state)
        grad_reset = grad_inner * carried * reset_gate * (1.0 - reset_gate)
        grad_gate_z = grad_update * update * (1.0 - update)
        grad_carried = grad_inner * reset_gate
        gate_grads.insert(0, jnp.concatenate([grad_reset, grad_gate_z, grad_inner], 1))
        rec_low = jnp.concatenate([grad_reset, grad_gate_z, grad_carried], 1).astype(jnp.bfloat16)
        weight_grad = weight_grad + product_tn(rec_low, prev_low)
        bias_grad = bias_grad + jnp.concatenate(
            [
                jnp.sum(grad_reset, 0),
                jnp.sum(grad_gate_z, 0),
                jnp.sum(grad_inner, 0),
                jnp.sum(grad_carried, 0),
            ]
        )
        grad_state = grad_prev + product(rec_low, rec_weight)
    return (jnp.stack(gate_grads, 1), weight_grad, bias_grad)


def per_device(
    tokens,
    char_ids,
    token_chars,
    groups,
    qkv_weight,
    out_weight,
    ffn_in,
    ffn_out,
    conv_weight,
    gains,
    ih_weight,
    hh_weight,
    gru_bias,
    char_table,
    group_table,
    token_cot,
    char_cot,
):
    seq_len = tokens.shape[0]
    model_width = tokens.shape[1]
    layer_full = (
        lax.all_gather(qkv_weight, "dp", axis=0, tiled=True),
        lax.all_gather(out_weight, "dp", axis=1, tiled=True),
        lax.all_gather(ffn_in, "dp", axis=0, tiled=True),
        lax.all_gather(ffn_out, "dp", axis=1, tiled=True),
        lax.all_gather(conv_weight, "dp", axis=0, tiled=True),
        lax.all_gather(gains, "dp", axis=1, tiled=True),
    )
    char_full = (
        lax.all_gather(ih_weight, ("dp", "mp"), axis=0, tiled=True),
        lax.all_gather(hh_weight, ("dp", "mp"), axis=0, tiled=True),
        lax.all_gather(gru_bias, ("dp", "mp"), axis=1, tiled=True),
        lax.all_gather(char_table, ("dp", "mp"), axis=1, tiled=True),
        lax.all_gather(group_table, ("dp", "mp"), axis=1, tiled=True),
    )
    qkv_full, out_full, in_full, down_full, conv_full, gain_full = layer_full
    ih_full, hh_full, bias_full, table_full, group_full = char_full
    local_width = out_full.shape[0]
    head_size = model_width // HEADS
    local_heads = local_width // head_size
    gain_rows = gain_full.astype(jnp.float32)
    qkv_mat = qkv_full.reshape(model_width, 3 * local_width)
    packed = (
        product(tokens, qkv_mat).astype(jnp.bfloat16).reshape(seq_len, 3, local_heads, head_size)
    )
    queries = packed[:, 0]
    key_rows = packed[:, 1]
    values = packed[:, 2]
    block_rows = min(512, seq_len)
    head_out, log_sum = attend_forward(queries, key_rows, values)
    log_sums = [log_sum]
    attn_low = head_out.reshape(seq_len, local_width).astype(jnp.bfloat16)
    first_sum = tokens.astype(jnp.float32) + lax.psum(
        product(attn_low, out_full).astype(jnp.bfloat16), "mp"
    ).astype(jnp.float32)
    normed_one = norm_rows(first_sum, gain_rows[0])
    normed_low = normed_one.astype(jnp.bfloat16)
    hidden_pre = product(normed_low, in_full)
    hidden = gelu_fn(hidden_pre).astype(jnp.bfloat16)
    second = normed_one + lax.psum(product(hidden, down_full).astype(jnp.bfloat16), "mp").astype(
        jnp.float32
    )
    normed_two = norm_rows(second, gain_rows[1])
    unit_count = hh_full.shape[1]
    gate_width = 3 * unit_count
    own_rows = seq_len // lax.axis_size("mp")
    mp_index = lax.axis_index("mp")
    counts = token_chars[0]
    starts = jnp.cumsum(counts) - counts
    own_counts = lax.dynamic_slice_in_dim(counts, mp_index * own_rows, own_rows)
    own_starts = lax.dynamic_slice_in_dim(starts, mp_index * own_rows, own_rows)
    slot_ids = jnp.arange(MAXC, dtype=jnp.int32)
    live_slots = (slot_ids[None, :] < own_counts[:, None]).astype(jnp.float32)
    forward_pos = own_starts[:, None] + jnp.minimum(slot_ids[None, :], own_counts[:, None] - 1)
    backward_pos = own_starts[:, None] + jnp.maximum(own_counts[:, None] - 1 - slot_ids[None, :], 0)
    group_row = lax.dynamic_index_in_dim(group_full, groups[0], 0, keepdims=False).astype(
        jnp.float32
    )
    letters = char_ids[0]
    embed_dim = table_full.shape[1]
    direction_runs = []
    finals = []
    for direction, positions in ((0, forward_pos), (1, backward_pos)):
        symbol_ids = letters[positions]
        embeds = (
            (table_full[symbol_ids].astype(jnp.float32) + group_row)
            .astype(jnp.bfloat16)
            .reshape(own_rows * MAXC, embed_dim)
        )
        in_weight = ih_full[:, direction * gate_width : (direction + 1) * gate_width]
        rec_weight = hh_full[direction * gate_width : (direction + 1) * gate_width]
        bias_row = bias_full[direction].astype(jnp.float32)
        gate_in = product(embeds, in_weight).reshape(own_rows, MAXC, gate_width)
        final_state, saved_steps = recur_forward(gate_in, rec_weight, bias_row, live_slots)
        direction_runs.append((symbol_ids, embeds, saved_steps))
        finals.append(final_state.astype(jnp.bfloat16))
    char_rows = lax.all_gather(jnp.concatenate(finals, 1), "mp", axis=0, tiled=True)
    mixed_rows = jnp.concatenate([normed_two.astype(jnp.bfloat16), char_rows], 1)
    earlier_rows = rows_earlier(mixed_rows)
    later_rows = rows_later(mixed_rows)
    conv_taps = conv_full.reshape(3, 2 * model_width, local_width)
    joined_pre = (
        product(earlier_rows, conv_taps[0])
        + product(mixed_rows, conv_taps[1])
        + product(later_rows, conv_taps[2])
    )
    joined_all = lax.all_gather(
        gelu_fn(joined_pre).astype(jnp.bfloat16), "mp", axis=1, tiled=True
    ).astype(jnp.float32)
    token_sum = normed_two + joined_all
    char_sum = char_rows.astype(jnp.float32) + joined_all
    token_out = norm_rows(token_sum, gain_rows[2])
    char_out = norm_rows(char_sum, gain_rows[3])
    fenced = lax.optimization_barrier(
        (
            qkv_weight,
            out_weight,
            ffn_in,
            ffn_out,
            conv_weight,
            gains,
            ih_weight,
            hh_weight,
            token_out,
        )
    )
    layer_back = (
        lax.all_gather(fenced[0], "dp", axis=0, tiled=True),
        lax.all_gather(fenced[1], "dp", axis=1, tiled=True),
        lax.all_gather(fenced[2], "dp", axis=0, tiled=True),
        lax.all_gather(fenced[3], "dp", axis=1, tiled=True),
        lax.all_gather(fenced[4], "dp", axis=0, tiled=True),
        lax.all_gather(fenced[5], "dp", axis=1, tiled=True),
    )
    char_back = (
        lax.all_gather(fenced[6], ("dp", "mp"), axis=0, tiled=True),
        lax.all_gather(fenced[7], ("dp", "mp"), axis=0, tiled=True),
    )
    ih_back = char_back[0]
    hh_back = char_back[1]
    qkv_back, out_back, in_back, down_back, conv_back, gain_back = layer_back
    gain_back_rows = gain_back.astype(jnp.float32)
    grad_token_sum, gain_grad_three = pull_back(
        norm_rows, (token_sum, gain_back_rows[2]), token_cot.astype(jnp.float32)
    )
    grad_char_sum, gain_grad_four = pull_back(
        norm_rows, (char_sum, gain_back_rows[3]), char_cot.astype(jnp.float32)
    )
    grad_joined = grad_token_sum + grad_char_sum
    grad_joined_own = lax.dynamic_slice_in_dim(grad_joined, mp_index * local_width, local_width, 1)
    grad_pre_low = pull_back(gelu_fn, (joined_pre,), grad_joined_own)[0].astype(jnp.bfloat16)
    conv_taps_back = conv_back.reshape(3, 2 * model_width, local_width)
    conv_grad = jnp.stack(
        [
            product_tn(earlier_rows, grad_pre_low),
            product_tn(mixed_rows, grad_pre_low),
            product_tn(later_rows, grad_pre_low),
        ]
    ).reshape(6 * model_width, local_width)
    grad_mixed_part = (
        product_nt(grad_pre_low, conv_taps_back[1])
        + rows_later(product_nt(grad_pre_low, conv_taps_back[0]))
        + rows_earlier(product_nt(grad_pre_low, conv_taps_back[2]))
    )
    grad_mixed = lax.psum(grad_mixed_part.astype(jnp.bfloat16), "mp").astype(jnp.float32)
    grad_normed_two = grad_token_sum + grad_mixed[:, :model_width]
    grad_char_rows = grad_char_sum + grad_mixed[:, model_width:]
    grad_second, gain_grad_two = pull_back(norm_rows, (second, gain_back_rows[1]), grad_normed_two)
    second_low = grad_second.astype(jnp.bfloat16)
    down_grad = product_tn(hidden, second_low)
    grad_hidden_low = pull_back(gelu_fn, (hidden_pre,), product_nt(second_low, down_back))[
        0
    ].astype(jnp.bfloat16)
    in_grad = product_tn(normed_low, grad_hidden_low)
    grad_normed_one = grad_second + lax.psum(
        product_nt(grad_hidden_low, in_back).astype(jnp.bfloat16), "mp"
    ).astype(jnp.float32)
    grad_first, gain_grad_one = pull_back(
        norm_rows, (first_sum, gain_back_rows[0]), grad_normed_one
    )
    first_low = grad_first.astype(jnp.bfloat16)
    out_grad = product_tn(attn_low, first_low)
    grad_attn = (
        product_nt(first_low, out_back)
        .astype(jnp.bfloat16)
        .reshape(seq_len, local_heads, head_size)
    )
    query_grads = []
    key_total = jnp.zeros(key_rows.shape, jnp.float32)
    value_total = jnp.zeros(values.shape, jnp.float32)
    for block_index, offset in enumerate(range(0, seq_len, block_rows)):
        query_grad, key_grad, value_grad = attend_backward(
            queries, key_rows, values, log_sums[block_index], grad_attn
        )
        query_grads.append(query_grad)
        key_total = key_grad
        value_total = value_grad
    grad_packed = (
        jnp.stack([query_grads[0], key_total, value_total], 1)
        .astype(jnp.bfloat16)
        .reshape(seq_len, 3 * local_width)
    )
    qkv_grad = product_tn(tokens, grad_packed).reshape(model_width, 3, local_width)
    qkv_mat_back = qkv_back.reshape(model_width, 3 * local_width)
    token_grad = grad_first + lax.psum(
        product_nt(grad_packed, qkv_mat_back).astype(jnp.bfloat16), "mp"
    ).astype(jnp.float32)
    grad_own = lax.dynamic_slice_in_dim(grad_char_rows, mp_index * own_rows, own_rows, 0)
    ih_parts = []
    hh_parts = []
    bias_parts = []
    table_grad = jnp.zeros((table_full.shape[0], embed_dim), jnp.float32)
    embed_total = jnp.zeros((embed_dim,), jnp.float32)
    for direction in (0, 1):
        symbol_ids, embeds, saved_steps = direction_runs[direction]
        in_weight = ih_back[:, direction * gate_width : (direction + 1) * gate_width]
        rec_weight = hh_back[direction * gate_width : (direction + 1) * gate_width]
        gate_grad, rec_weight_grad, bias_grad_row = recur_backward(
            grad_own[:, direction * unit_count : (direction + 1) * unit_count],
            saved_steps,
            rec_weight,
            live_slots,
        )
        gate_low = gate_grad.astype(jnp.bfloat16).reshape(own_rows * MAXC, gate_width)
        ih_parts.append(product_tn(embeds, gate_low))
        embed_grad = product_nt(gate_low, in_weight)
        table_grad = table_grad + jax.ops.segment_sum(
            embed_grad, symbol_ids.reshape(-1), num_segments=table_grad.shape[0]
        )
        embed_total = embed_total + jnp.sum(embed_grad, 0)
        hh_parts.append(rec_weight_grad)
        bias_parts.append(bias_grad_row)
    group_hit = (jnp.arange(group_full.shape[0], dtype=jnp.int32) == groups[0]).astype(jnp.float32)
    group_grad = group_hit[:, None] * embed_total[None, :]
    ih_grad = jnp.concatenate(ih_parts, 1)
    hh_grad = jnp.concatenate(hh_parts, 0)
    bias_grad = jnp.stack(bias_parts)
    gain_grad = jnp.stack([gain_grad_one, gain_grad_two, gain_grad_three, gain_grad_four])
    layer_grads = (
        lax.psum_scatter(qkv_grad, "dp", scatter_dimension=0, tiled=True),
        lax.psum_scatter(out_grad, "dp", scatter_dimension=1, tiled=True),
        lax.psum_scatter(in_grad, "dp", scatter_dimension=0, tiled=True),
        lax.psum_scatter(down_grad, "dp", scatter_dimension=1, tiled=True),
        lax.psum_scatter(conv_grad, "dp", scatter_dimension=0, tiled=True),
        lax.psum_scatter(gain_grad, "dp", scatter_dimension=1, tiled=True),
    )
    char_grads = (
        lax.psum_scatter(ih_grad, ("dp", "mp"), scatter_dimension=0, tiled=True),
        lax.psum_scatter(hh_grad, ("dp", "mp"), scatter_dimension=0, tiled=True),
        lax.psum_scatter(bias_grad, ("dp", "mp"), scatter_dimension=1, tiled=True),
        lax.psum_scatter(table_grad, ("dp", "mp"), scatter_dimension=1, tiled=True),
        lax.psum_scatter(group_grad, ("dp", "mp"), scatter_dimension=1, tiled=True),
    )
    return (
        token_out.astype(jnp.bfloat16),
        char_out.astype(jnp.bfloat16),
        token_grad,
        layer_grads[0],
        layer_grads[1],
        layer_grads[2],
        layer_grads[3],
        layer_grads[4],
        layer_grads[5],
        char_grads[0],
        char_grads[1],
        char_grads[2],
        char_grads[3],
        char_grads[4],
    )


def solution(mesh):
    return jax.shard_map(
        per_device,
        mesh=mesh,
        in_specs=(
            P("dp", None),
            P("dp", None),
            P("dp", None),
            P("dp"),
            P("dp", None, "mp"),
            P("mp", "dp"),
            P("dp", "mp"),
            P("mp", "dp"),
            P("dp", "mp"),
            P(None, "dp"),
            P(("dp", "mp"), None),
            P(("dp", "mp"), None),
            P(None, ("dp", "mp")),
            P(None, ("dp", "mp")),
            P(None, ("dp", "mp")),
            P("dp", None),
            P("dp", None),
        ),
        out_specs=(
            P("dp", None),
            P("dp", None),
            P("dp", None),
            P("dp", None, "mp"),
            P("mp", "dp"),
            P("dp", "mp"),
            P("mp", "dp"),
            P("dp", "mp"),
            P(None, "dp"),
            P(("dp", "mp"), None),
            P(("dp", "mp"), None),
            P(None, ("dp", "mp")),
            P(None, ("dp", "mp")),
            P(None, ("dp", "mp")),
        ),
        check_vma=False,
    )
```

profile of v0, /device:TPU:0, one launch (start us, length us, event | category | flops | bytes accessed | tf_op | source)
XLA Modules:
  0.0 1365.0 jit_solution(4899108975177223401)
XLA Ops:
  9.1 14.6 %all_gather.63 = bf16[768,3,192]{2,1,0:T(4,128)(2,1)S(1)} all-gather(bf16[96,3,192]{2,1,0:T(4,128)(2,1)S(1)} %copy.147), channel_id=1, replica_groups=mesh['dp'=8,'mp'=4] {'dp'}, dimensions={0}, use_global_device_ids=true | all-gather | bytes 995328 | tf_op jit(solution)/shard_map/all_gather | solution.py:172
  28.1 8.5 all_gather.64
  39.6 9.0 all-gather
  49.3 28.3 %all-reduce.12.cloned.1.call-done = bf16[384,768]{1,0:T(8,128)(2,1)} async-done(((bf16[384,768]{1,0:T(8,128)(2,1)}), bf16[384,768]{1,0:T(8,128)(2,1)}) %all-reduce.12.cloned.1.call-update) | async-done | bytes 589840 | tf_op jit(solution)/shard_map/psum | solution.py:203
  83.0 7.1 all-gather.18.cloned.1.call-done
  96.0 4.5 gather_fusion
  100.7 73.4 %all_gather.68 = bf16[1000,256]{0,1:T(8,128)(2,1)S(1)} all-gather(bf16[1000,8]{0,1:T(8,128)(2,1)S(1)} %copy-done.350), channel_id=1, replica_groups=mesh['dp'=8,'mp'=4] {'dp','mp'}, dimensions={1}, use_global_device_ids=true | all-gather | bytes 528000 | tf_op jit(solution)/shard_map/all_gather | solution.py:183
  178.5 63.0 %all-gather.1 = bf16[32,48,2]{1,2,0:T(2,128)(2,1)S(1)} all-gather(bf16[1,48,2]{1,2,0:T(2,128)(2,1)S(1)} %bitcast.294), channel_id=1, replica_groups=mesh['dp'=8,'mp'=4] {'dp','mp'}, dimensions={0}, use_global_device_ids=true | all-gather | bytes 6336 | tf_op jit(solution)/shard_map/all_gather | solution.py:182
  242.4 4.5 gather_fusion.2
  251.0 66.6 %all_gather.69 = bf16[16,256]{0,1:T(8,128)(2,1)S(1)} all-gather(bf16[16,8]{0,1:T(8,128)(2,1)} %param.31), channel_id=1, replica_groups=mesh['dp'=8,'mp'=4] {'dp','mp'}, dimensions={1}, use_global_device_ids=true | all-gather | bytes 8448 | tf_op jit(solution)/shard_map/all_gather | solution.py:184
  333.6 4.1 reshape.1390
  362.0 27.1 %all_gather.73 = bf16[384,768]{1,0:T(8,128)(2,1)S(1)} all-gather(bf16[96,768]{1,0:T(8,128)(2,1)S(1)} %pad_maximum_fusion.20), channel_id=1, replica_groups=mesh['dp'=8,'mp'=4] {'mp'}, dimensions={0}, use_global_device_ids=true | all-gather | bytes 737280 | tf_op jit(solution)/shard_map/all_gather | solution.py:247
  395.8 15.8 %all_gather.75 = bf16[384,768]{0,1:T(8,128)(2,1)} all-gather(bf16[384,192]{0,1:T(8,128)(2,1)} %copy.179), channel_id=1, replica_groups=mesh['dp'=8,'mp'=4] {'mp'}, dimensions={1}, use_global_device_ids=true | all-gather | bytes 737280 | tf_op jit(solution)/shard_map/all_gather | solution.py:257
  419.5 10.9 all-gather.3
  444.6 11.1 all-gather.34.cloned.1.call-done
  470.8 52.9 %all-reduce.16.cloned.1.call-done = bf16[384,1536]{1,0:T(8,128)(2,1)} async-done(((bf16[384,1536]{1,0:T(8,128)(2,1)}), bf16[384,1536]{1,0:T(8,128)(2,1)}) %all-reduce.16.cloned.1.call-update) | async-done | bytes 1179664 | tf_op jit(solution)/shard_map/psum | solution.py:315
  544.4 14.9 %all_gather.81 = bf16[768,3,192]{2,1,0:T(4,128)(2,1)} all-gather(bf16[96,3,192]{2,1,0:T(4,128)(2,1)S(1)} %copy.187), channel_id=1, replica_groups=mesh['dp'=8,'mp'=4] {'dp'}, dimensions={0}, use_global_device_ids=true | all-gather | bytes 995328 | tf_op jit(solution)/shard_map/all_gather | solution.py:278
  569.9 12.3 all-gather.28.cloned.1.call-done
  619.5 11.8 all_gather.80
  631.3 5.5 copy.215
  662.4 7.2 scatter_custom_fusion.1
  676.2 7.4 scatter_custom_fusion
  727.1 40.0 %all-reduce.5 = f32[16,256]{0,1:T(8,128)S(1)} all-reduce(f32[16,256]{0,1:T(8,128)S(1)} %broadcast_multiply_fusion), channel_id=12, replica_groups=mesh['dp'=8,'mp'=4] {'dp','mp'}, use_global_device_ids=true, to_apply=%region_108.109.clone | all-reduce | flops 4096 | bytes 32768
  769.1 6.0 reduce-scatter.35.cloned.1.call-done
  776.6 55.7 %reduce-scatter.33.cloned.1.call-done = f32[576,192]{1,0:T(8,128)} async-done(((f32[4608,192]{1,0:T(8,128)}), f32[576,192]{1,0:T(8,128)}) %reduce-scatter.33.cloned.1.call-update) | async-done | bytes 442384
  836.6 34.1 %reduce-scatter.31.cloned.1.call-done = f32[96,192]{1,0:T(8,128)} async-done(((f32[768,192]{1,0:T(8,128)}), f32[96,192]{1,0:T(8,128)}) %reduce-scatter.31.cloned.1.call-update) | async-done | bytes 73744
  872.3 136.8 %reduce-scatter.39.cloned.1.call-done = f32[8,1000]{1,0:T(8,128)} async-done(((f32[256,1000]{1,0:T(8,128)}), f32[8,1000]{1,0:T(8,128)}) %reduce-scatter.39.cloned.1.call-update) | async-done | bytes 32016
  1009.2 101.1 %reduce-scatter.29.cloned.1.call-done = f32[8,2304]{1,0:T(8,128)} async-done(((f32[256,2304]{1,0:T(8,128)}), f32[8,2304]{1,0:T(8,128)}) %reduce-scatter.29.cloned.1.call-update) | async-done | bytes 73744 | tf_op jit(solution)/shard_map/reduce_scatter | solution.py:398
  1110.3 45.7 %reduce-scatter.23.cloned.1.call-done = f32[96,3,192]{2,0,1:T(8,128)} async-done(((f32[768,3,192]{2,0,1:T(8,128)}), f32[96,3,192]{2,0,1:T(8,128)}) %reduce-scatter.23.cloned.1.call-update) | async-done | bytes 221200 | tf_op jit(solution)/shard_map/reduce_scatter | solution.py:390
  1155.9 46.3 %reduce-scatter.27.cloned.1.call-done = f32[768,96]{0,1:T(8,128)} async-done(((f32[768,768]{0,1:T(8,128)}), f32[768,96]{0,1:T(8,128)}) %reduce-scatter.27.cloned.1.call-update) | async-done | bytes 294928 | tf_op jit(solution)/shard_map/reduce_scatter | solution.py:393
  1202.2 46.5 %reduce-scatter.25.cloned.1.call-done = f32[96,768]{1,0:T(8,128)} async-done(((f32[768,768]{1,0:T(8,128)}), f32[96,768]{1,0:T(8,128)}) %reduce-scatter.25.cloned.1.call-update) | async-done | bytes 294928 | tf_op jit(solution)/shard_map/reduce_scatter | solution.py:392
  1248.7 108.9 %reduce-scatter.41.cloned.1.call-done = f32[72,384]{1,0:T(8,128)} async-done(((f32[2304,384]{1,0:T(8,128)}), f32[72,384]{1,0:T(8,128)}) %reduce-scatter.41.cloned.1.call-update) | async-done | bytes 110608
  (1144 shorter events, 262.0 us)
Async XLA Ops:
  8.0 87.9 %copy-start = (s32[1,1536]{1,0:T(1,128)S(1)}, s32[1,1536]{1,0:T(1,128)}, u32[]{:S(2)}) copy-start(s32[1,1536]{1,0:T(1,128)} %param.18) | copy-start | bytes 18436
  8.0 69.6 %all-reduce.12.cloned.1.call-start = ((), (), s32[]{:S(2)}) async-start(), calls=%async_computation.10 | async-start | bytes 1179648 | tf_op jit(solution)/shard_map/psum | solution.py:203
  37.8 42.2 %all-gather.16.cloned.1.call-start = ((), (), s32[]{:S(2)}) async-start(), calls=%async_computation.11 | async-start | bytes 1327104 | tf_op jit(solution)/shard_map/all_gather | solution.py:174
  38.4 51.7 %all-gather.18.cloned.1.call-start = ((), (), s32[]{:S(2)}) async-start(), calls=%async_computation.12 | async-start | bytes 1327104 | tf_op jit(solution)/shard_map/all_gather | solution.py:175
  39.0 279.8 %all-gather.20.cloned.1.call-start = ((), (), s32[]{:S(2)}) async-start(), calls=%async_computation.14 | async-start | bytes 1216512 | tf_op jit(solution)/shard_map/all_gather | solution.py:180
  39.6 285.8 %all-reduce.14.cloned.1.call-start = ((), (), s32[]{:S(2)}) async-start(), calls=%async_computation.13 | async-start | bytes 1179648 | tf_op jit(solution)/shard_map/psum | solution.py:210
  49.3 30.7 %copy-start.323 = (f32[768]{0:T(1024)}, f32[768]{0:T(1024)S(1)}, u32[]{:S(2)}) copy-start(f32[768]{0:T(1024)S(1)} %get-tuple-element.119) | copy-start | bytes 9220
  93.4 236.2 %all-gather.32.cloned.1.call-start = ((), (), s32[]{:S(2)}) async-start(), calls=%async_computation.27 | async-start | bytes 2211840 | tf_op jit(solution)/shard_map/all_gather | solution.py:176
  94.1 243.6 %all-gather.22.cloned.1.call-start = ((), (), s32[]{:S(2)}) async-start(), calls=%async_computation.15 | async-start | bytes 1824768 | tf_op jit(solution)/shard_map/all_gather | solution.py:181
  94.9 360.9 %all-gather.34.cloned.1.call-start = ((), (), s32[]{:S(2)}) async-start(), calls=%async_computation.28 | async-start | bytes 2211840 | tf_op jit(solution)/shard_map/all_gather | solution.py:282
  251.0 67.8 %copy-start.24 = (f32[96,8,256]{2,1,0:T(8,128)S(1)}, f32[96,8,256]{2,1,0:T(8,128)}, u32[]{:S(2)}) copy-start(f32[96,8,256]{2,1,0:T(8,128)} %bitcast_convert_fusion.1) | copy-start | bytes 2359300
  361.1 28.1 %copy-start.86 = (bf16[384,768]{1,0:T(8,128)(2,1)S(1)}, bf16[384,768]{1,0:T(8,128)(2,1)}, u32[]{:S(2)}) copy-start(bf16[384,768]{1,0:T(8,128)(2,1)} %multiply_convert_fusion.3) | copy-start | bytes 1769476
  430.4 93.3 %all-reduce.16.cloned.1.call-start = ((), (), s32[]{:S(2)}) async-start(), calls=%async_computation.16 | async-start | bytes 2359296 | tf_op jit(solution)/shard_map/psum | solution.py:315
  467.7 60.3 %all-gather.24.cloned.1.call-start = ((), (), s32[]{:S(2)}) async-start(), calls=%async_computation.17 | async-start | bytes 1327104 | tf_op jit(solution)/shard_map/all_gather | solution.py:281
  468.3 63.4 %all-gather.26.cloned.1.call-start = ((), (), s32[]{:S(2)}) async-start(), calls=%async_computation.18 | async-start | bytes 1327104 | tf_op jit(solution)/shard_map/all_gather | solution.py:280
  468.9 113.2 %all-gather.28.cloned.1.call-start = ((), (), s32[]{:S(2)}) async-start(), calls=%async_computation.24 | async-start | bytes 1824768 | tf_op jit(solution)/shard_map/all_gather | solution.py:287
  469.5 144.8 %all-reduce.18.cloned.1.call-start = ((), (), s32[]{:S(2)}) async-start(), calls=%async_computation.19 | async-start | bytes 1179648 | tf_op jit(solution)/shard_map/psum | solution.py:325
  534.8 120.4 %all-gather.30.cloned.1.call-start = ((), (), s32[]{:S(2)}) async-start(), calls=%async_computation.26 | async-start | bytes 1216512 | tf_op jit(solution)/shard_map/all_gather | solution.py:286
  544.4 15.4 %copy-start.30 = (f32[1,1536,192]{1,2,0:T(8,128)S(1)}, f32[1,1536,192]{1,2,0:T(8,128)}, u32[]{:S(2)}) copy-start(f32[1,1536,192]{1,2,0:T(8,128)} %convolution_bitcast_fusion.4) | copy-start | bytes 3538948
  559.3 208.4 %reduce-scatter.37.cloned.1.call-start = ((), (), s32[]{:S(2)}) async-start(), calls=%async_computation.32 | async-start | bytes 811008
  614.2 160.9 %reduce-scatter.35.cloned.1.call-start = ((), (), s32[]{:S(2)}) async-start(), calls=%async_computation.31 | async-start | bytes 442368
  619.4 212.8 %reduce-scatter.33.cloned.1.call-start = ((), (), s32[]{:S(2)}) async-start(), calls=%async_computation.30 | async-start | bytes 5308416
  640.2 194.1 %all-reduce.20.cloned.1.call-start = ((), (), s32[]{:S(2)}) async-start(), calls=%async_computation.20 | async-start | bytes 1179648 | tf_op jit(solution)/shard_map/psum | solution.py:355
  654.4 216.3 %reduce-scatter.31.cloned.1.call-start = ((), (), s32[]{:S(2)}) async-start(), calls=%async_computation.29 | async-start | bytes 884736
  660.7 348.5 %reduce-scatter.39.cloned.1.call-start = ((), (), s32[]{:S(2)}) async-start(), calls=%async_computation.33 | async-start | bytes 1081344
  688.9 421.4 %reduce-scatter.29.cloned.1.call-start = ((), (), s32[]{:S(2)}) async-start(), calls=%async_computation.25 | async-start | bytes 2433024 | tf_op jit(solution)/shard_map/reduce_scatter | solution.py:398
  694.1 461.9 %reduce-scatter.23.cloned.1.call-start = ((), (), s32[]{:S(2)}) async-start(), calls=%async_computation.21 | async-start | bytes 2654208 | tf_op jit(solution)/shard_map/reduce_scatter | solution.py:390
  698.9 503.3 %reduce-scatter.27.cloned.1.call-start = ((), (), s32[]{:S(2)}) async-start(), calls=%async_computation.23 | async-start | bytes 2654208 | tf_op jit(solution)/shard_map/reduce_scatter | solution.py:393
  703.6 545.2 %reduce-scatter.25.cloned.1.call-start = ((), (), s32[]{:S(2)}) async-start(), calls=%async_computation.22 | async-start | bytes 2654208 | tf_op jit(solution)/shard_map/reduce_scatter | solution.py:392
  713.6 644.0 %reduce-scatter.41.cloned.1.call-start = ((), (), s32[]{:S(2)}) async-start(), calls=%async_computation.34 | async-start | bytes 3649536
  726.4 107.9 %copy-start.332 = (f32[384]{0:T(512)S(1)}, f32[384]{0:T(512)}, u32[]{:S(2)}) copy-start(f32[384]{0:T(512)} %copy-done.330) | copy-start | bytes 4612
  832.2 525.4 %copy-start.1 = (s32[1,1536]{1,0:T(1,128)S(1)}, s32[1,1536]{1,0:T(1,128)}, u32[]{:S(2)}) copy-start(s32[1,1536]{1,0:T(1,128)} %param.18) | copy-start | bytes 18436
  (377 other events, 748.5 us)
Sparse Core Ops, SparseCore 0:
  37.9 39.6 all-reduce.11
  93.5 43.2 all-reduce.13
  467.8 55.8 all-reduce.15
  534.9 40.9 all-reduce.17
  654.5 38.0 all-reduce.19
Sparse Core Ops, SparseCore 1:
  40.2 24.2 all-gather.15
  66.2 23.9 all-gather.17
  92.8 59.3 all-gather.19
  154.1 26.6 all-gather.31
  183.6 55.6 all-gather.21
  430.5 25.2 all-gather.33
  470.1 23.9 all-gather.23
  495.7 23.9 all-gather.25
  522.4 59.7 all-gather.27
  585.0 53.8 all-gather.29
  643.8 94.6 reduce-scatter.36
  742.1 32.9 reduce-scatter.34
  778.4 53.7 reduce-scatter.32
  835.7 34.9 reduce-scatter.30
  873.6 135.5 reduce-scatter.38
  1015.0 95.2 reduce-scatter.28
  1114.6 41.3 reduce-scatter.22
  1159.9 42.3 reduce-scatter.26
  1206.4 42.3 reduce-scatter.24
  1254.8 102.8 reduce-scatter.40
where the time goes:
time: 1370 us; the launch traced here: 1360 us
  waiting for transfers between devices  698 us (51%)
  blocking collectives  356 us (26%)
  local copies, waits for them, and re-layouts  105 us (8%)
  other arithmetic  95.6 us (7%)
  matrix products  87.8 us (6%)
  between operations  21.1 us (2%)
    unnamed x31, waiting for transfers between devices  346 us
    reduce_scatter x1, waiting for transfers between devices, per_device(): lax.psum_scatter(ih_grad, ('dp', 'mp'), scatter_dimension=0, tiled=True)  101 us
    all_gather x1, blocking collectives, per_device(): lax.all_gather(char_table, ('dp', 'mp'), axis=1, tiled=True)  73.4 us
    all_gather x1, blocking collectives, per_device(): lax.all_gather(group_table, ('dp', 'mp'), axis=1, tiled=True)  66.6 us
    all_gather x1, blocking collectives, per_device(): lax.all_gather(gru_bias, ('dp', 'mp'), axis=1, tiled=True)  63 us
    unnamed x782, local copies, waits for them, and re-layouts  58.4 us
    psum x1, waiting for transfers between devices, per_device(): lax.psum(grad_mixed_part.astype(jnp.bfloat16), 'mp').astype(jnp.float32)  52.9 us
    reduce_scatter x1, waiting for transfers between devices, per_device(): lax.psum_scatter(in_grad, 'dp', scatter_dimension=0, tiled=True)  46.5 us
  transfers between devices with their start and end apart: 25, of which 14 were waited for; matrix products, arithmetic and copies ran while one was open for 15% of the time, Pallas kernels for 0%

commit v1 on v0

v1 whole, which is shorter than its diff:
```python
import jax
import jax.numpy as jnp
from jax import lax
from jax.experimental import pallas as pl
from jax.experimental.pallas import tpu as pltpu
from jax.sharding import PartitionSpec as P

HEADS = 12
MAXC = 8
NORM_EPS = 1e-05
BF = jnp.bfloat16
F32 = jnp.float32
GROUP_LANE = 96
MB = 1 << 20


def dot(left, right, dims):
    return lax.dot_general(left, right, (dims, ((), ())), preferred_element_type=F32)


def product(left, right):
    return dot(left, right, ((1,), (0,)))


def product_tn(left, right):
    return dot(left, right, ((0,), (0,)))


def product_nt(left, right):
    return dot(left, right, ((1,), (1,)))


def swap(rows, axis, mask):
    size = lax.axis_size(axis)
    return lax.ppermute(rows, axis, [(i, i ^ mask) for i in range(size)])


def place(blocks, where, count, axis=0):
    number = len(blocks)
    first = blocks[0]
    shape = first.shape[:axis] + (count,) + first.shape[axis:]

    def body(where_ref, *refs):
        out, sems = refs[number], refs[number + 1]
        copies = [
            pltpu.make_async_copy(
                refs[i], out.at[(slice(None),) * axis + (where_ref[i],)], sems.at[i]
            )
            for i in range(number)
        ]
        for copy in copies:
            copy.start()
        for copy in copies:
            copy.wait()

    return pl.pallas_call(
        body,
        out_shape=jax.ShapeDtypeStruct(shape, first.dtype),
        in_specs=[pl.BlockSpec(memory_space=pltpu.SMEM)]
        + [pl.BlockSpec(memory_space=pl.ANY)] * number,
        out_specs=pl.BlockSpec(memory_space=pl.ANY),
        scratch_shapes=[pltpu.SemaphoreType.DMA((number,))],
        compiler_params=pltpu.CompilerParams(vmem_limit_bytes=MB),
    )(jnp.stack(where).astype(jnp.int32), *blocks)


def quick():
    return lax.axis_size("dp") == 8


def gather_mp(rows):
    size, own = lax.axis_size("mp"), lax.axis_index("mp")
    blocks = [rows] + [swap(rows, "mp", mask) for mask in range(1, size)]
    return place(blocks, [own ^ mask for mask in range(size)], size)


def gather_dp_from(blocks_of, axis):
    size, own = lax.axis_size("dp"), lax.axis_index("dp")
    masks = list(range(0, size, 2))
    blocks = [blocks_of] + [swap(blocks_of, "dp", mask) for mask in masks[1:]]
    other = [swap(block, "dp", 1) for block in blocks]
    where = [own ^ mask for mask in masks] + [own ^ mask ^ 1 for mask in masks]
    return place(blocks + other, where, size, axis)


def gather_dp(rows, axis=0):
    if not quick():
        return lax.all_gather(rows, "dp", axis=axis)
    return gather_dp_from(rows, axis)


def gather_all(rows):
    if not quick():
        full = lax.all_gather(rows, ("dp", "mp"), axis=0)
        return full.reshape((lax.axis_size("dp"), lax.axis_size("mp")) + rows.shape)
    return gather_dp_from(gather_mp(rows), 0)


def take(blocks, index, axis=0):
    return lax.dynamic_index_in_dim(blocks, index, axis, keepdims=False)


def scatter_mp(blocks):
    size, own = lax.axis_size("mp"), lax.axis_index("mp")
    total = take(blocks, own).astype(F32)
    for mask in range(1, size):
        total = total + swap(take(blocks, own ^ mask), "mp", mask).astype(F32)
    return total


def scatter_dp(blocks):
    size, own = lax.axis_size("dp"), lax.axis_index("dp")
    if not quick():
        return lax.psum_scatter(blocks.astype(F32), "dp", scatter_dimension=0)
    core, chip = own & 1, own >> 1
    pairs = blocks.reshape((size // 2, 2) + blocks.shape[1:])
    got = swap(take(pairs, 1 - core, 1), "dp", 1)
    both = (take(pairs, core, 1).astype(F32) + got.astype(F32)).astype(BF)
    total = take(both, chip).astype(F32)
    for mask in range(1, size // 2):
        total = total + swap(take(both, chip ^ mask), "dp", 2 * mask).astype(F32)
    return total


def norm_parts(rows_in):
    row_mean = jnp.mean(rows_in, axis=-1, keepdims=True)
    centred = rows_in - row_mean
    spread = jnp.mean(centred * centred, axis=-1, keepdims=True)
    scale = lax.rsqrt(spread + NORM_EPS)
    return centred * scale, scale


def norm_back(normal, scale, gain_row, cotangent):
    lifted = cotangent * gain_row
    inner = jnp.mean(lifted * normal, axis=-1, keepdims=True)
    grad = scale * (lifted - jnp.mean(lifted, axis=-1, keepdims=True) - normal * inner)
    return grad, jnp.sum(cotangent * normal, axis=0)


GELU_A = 0.7978845608028654
GELU_B = 0.044715


def gelu_fn(v):
    return 0.5 * v * (1.0 + jnp.tanh(GELU_A * (v + GELU_B * v * v * v)))


def gelu_grad(v):
    t = jnp.tanh(GELU_A * (v + GELU_B * v * v * v))
    return 0.5 * (1.0 + t) + 0.5 * v * (1.0 - t * t) * GELU_A * (1.0 + 3.0 * GELU_B * v * v)


def rows_earlier(rows_in):
    return jnp.concatenate([jnp.zeros_like(rows_in[:1]), rows_in[:-1]], 0)


def rows_later(rows_in):
    return jnp.concatenate([rows_in[1:], jnp.zeros_like(rows_in[:1])], 0)


def attend_forward(query_rows, key_rows, values):
    scores = (
        jnp.einsum("qhd,khd->hqk", query_rows, key_rows, preferred_element_type=F32) * 0.125
    )
    peak_score = jnp.max(scores, axis=-1, keepdims=True)
    raised = jnp.exp(scores - peak_score)
    row_total = jnp.sum(raised, axis=-1, keepdims=True)
    attn_probs = (raised / row_total).astype(BF)
    head_out = jnp.einsum("hqk,khd->qhd", attn_probs, values, preferred_element_type=F32)
    return head_out, (peak_score + jnp.log(row_total))[..., 0]


def attend_backward(query_rows, key_rows, values, log_sum, grad_out):
    scores = (
        jnp.einsum("qhd,khd->hqk", query_rows, key_rows, preferred_element_type=F32) * 0.125
    )
    attn_probs = jnp.exp(scores - log_sum[..., None])
    grad_probs = jnp.einsum("qhd,khd->hqk", grad_out, values, preferred_element_type=F32)
    inner_sum = jnp.sum(grad_probs * attn_probs, axis=-1, keepdims=True)
    grad_scores = (attn_probs * (grad_probs - inner_sum)).astype(BF)
    query_grad = 0.125 * jnp.einsum(
        "hqk,khd->qhd", grad_scores, key_rows, preferred_element_type=F32
    )
    key_grad = 0.125 * jnp.einsum(
        "hqk,qhd->khd", grad_scores, query_rows, preferred_element_type=F32
    )
    value_grad = jnp.einsum(
        "hqk,qhd->khd", attn_probs.astype(BF), grad_out, preferred_element_type=F32
    )
    return query_grad, key_grad, value_grad


def sigmoid(v):
    return 0.5 * jnp.tanh(0.5 * v) + 0.5


def one_hot(symbols, group, lanes, table_lanes):
    lane = lax.broadcasted_iota(jnp.int32, (symbols.shape[0], lanes), 1)
    hit = (lane == symbols) | (lane == table_lanes + GROUP_LANE + group)
    return hit.astype(F32).astype(BF)


def encoder_forward(symbols, group, char_pack, hh_full, bias_full, live, table_lanes):
    _, own_rows, _ = live.shape
    units = hh_full.shape[1]
    width = 3 * units
    lanes = table_lanes + 128
    embed = char_pack.shape[0]
    saved_shape = jax.ShapeDtypeStruct((2, MAXC, own_rows, units), BF)

    def body(group_ref, sym, pack, hh, bias, alive, final, emb, prev, rst, upd, car, fre, state):
        for way in range(2):
            hits = one_hot(sym[way], group_ref[0], lanes, table_lanes)
            rows = product_nt(hits, pack[:, 2 * width :]).astype(BF)
            emb[way] = rows.reshape(MAXC, own_rows, embed)
        state[...] = jnp.zeros_like(state)

        @pl.loop(0, MAXC)
        def _(slot):
            live_col = alive[slot]
            for way in range(2):
                hidden = state[way]
                low = hidden.astype(BF)
                prev[way, slot] = low
                gate = product(emb[way, slot], pack[:, way * width : (way + 1) * width])
                rec = product_nt(low, hh[way * width : (way + 1) * width])
                b_r = bias[way : way + 1, :units]
                b_z = bias[way : way + 1, units : 2 * units]
                b_n = bias[way : way + 1, 2 * units : 3 * units]
                b_c = bias[way : way + 1, 3 * units :]
                reset = sigmoid(gate[:, :units] + b_r + rec[:, :units])
                update = sigmoid(gate[:, units : 2 * units] + b_z + rec[:, units : 2 * units])
                carried = rec[:, 2 * units :] + b_c
                fresh = jnp.tanh(gate[:, 2 * units :] + b_n + reset * carried)
                rst[way, slot] = reset.astype(BF)
                upd[way, slot] = update.astype(BF)
                car[way, slot] = carried.astype(BF)
                fre[way, slot] = fresh.astype(BF)
                moved = (1.0 - update) * fresh + update * hidden
                state[way] = hidden + live_col * (moved - hidden)

        for way in range(2):
            final[:, way * units : (way + 1) * units] = state[way].astype(BF)

    vmem = pl.BlockSpec(memory_space=pltpu.VMEM)
    return pl.pallas_call(
        body,
        out_shape=[
            jax.ShapeDtypeStruct((own_rows, 2 * units), BF),
            jax.ShapeDtypeStruct((2, MAXC, own_rows, embed), BF),
        ]
        + [saved_shape] * 5,
        in_specs=[pl.BlockSpec(memory_space=pltpu.SMEM)] + [vmem] * 5,
        out_specs=[vmem] * 7,
        scratch_shapes=[pltpu.VMEM((2, own_rows, units), F32)],
        compiler_params=pltpu.CompilerParams(vmem_limit_bytes=40 * MB),
    )(group, symbols, char_pack, hh_full, bias_full, live)


def encoder_backward(
    grad_final, symbols, group, char_pack, hh_full, live, embeds, saved, table_lanes
):
    own_rows = live.shape[1]
    units = hh_full.shape[1]
    width = 3 * units
    lanes = table_lanes + 128
    embed = char_pack.shape[0]
    count = MAXC * own_rows

    def body(
        group_ref, grad_in, sym, pack, hh, alive, emb, prev, rst, upd, car, fre,
        pack_grad, hh_grad, bias_grad, grad, low, inner_low, sums,
    ):
        for way in range(2):
            grad[way] = grad_in[:, way * units : (way + 1) * units]
        sums[...] = jnp.zeros_like(sums)

        @pl.loop(0, MAXC)
        def _(step):
            slot = MAXC - 1 - step
            live_col = alive[slot]
            at = pl.ds(pl.multiple_of(slot * own_rows, 16), own_rows)
            for way in range(2):
                before = prev[way, slot].astype(F32)
                reset = rst[way, slot].astype(F32)
                update = upd[way, slot].astype(F32)
                carried = car[way, slot].astype(F32)
                fresh = fre[way, slot].astype(F32)
                g = grad[way]
                moved = live_col * g
                grad_fresh = moved * (1.0 - update)
                grad_update = moved * (before - fresh)
                grad_inner = grad_fresh * (1.0 - fresh * fresh)
                grad_carried = grad_inner * reset
                grad_reset = grad_carried * carried * (1.0 - reset)
                grad_z = grad_update * update * (1.0 - update)
                sums[way, 0] += grad_reset
                sums[way, 1] += grad_z
                sums[way, 2] += grad_inner
                sums[way, 3] += grad_carried
                low[way, at, :units] = grad_reset.astype(BF)
                low[way, at, units : 2 * units] = grad_z.astype(BF)
                low[way, at, 2 * units :] = grad_carried.astype(BF)
                inner_low[way, at, :] = grad_inner.astype(BF)
                back = product(low[way, at, :], hh[way * width : (way + 1) * width])
                grad[way] = g - moved + moved * update + back

        table_total = jnp.zeros((embed, lanes), F32)
        for way in range(2):
            for part in range(4):
                bias_grad[way, part : part + 1, :] = jnp.sum(sums[way, part], 0, keepdims=True)
            rows = emb[way].reshape(count, embed)
            gates = low[way, :, : 2 * units]
            inner = inner_low[way]
            left = way * width
            pack_grad[:, left : left + 2 * units] = product_tn(rows, gates).astype(BF)
            pack_grad[:, left + 2 * units : left + width] = product_tn(rows, inner).astype(BF)
            embed_grad = product_nt(gates, pack[:, left : left + 2 * units]) + product_nt(
                inner, pack[:, left + 2 * units : left + width]
            )
            hits = one_hot(sym[way], group_ref[0], lanes, table_lanes)
            table_total = table_total + product_tn(embed_grad.astype(BF), hits)
            hh_grad[left : left + width] = product_tn(
                low[way], prev[way].reshape(count, units)
            ).astype(BF)
        pack_grad[:, 2 * width :] = table_total.astype(BF)

    vmem = pl.BlockSpec(memory_space=pltpu.VMEM)
    return pl.pallas_call(
        body,
        out_shape=[
            jax.ShapeDtypeStruct(char_pack.shape, BF),
            jax.ShapeDtypeStruct(hh_full.shape, BF),
            jax.ShapeDtypeStruct((2, 4, units), F32),
        ],
        in_specs=[pl.BlockSpec(memory_space=pltpu.SMEM)] + [vmem] * 11,
        out_specs=[vmem] * 3,
        scratch_shapes=[
            pltpu.VMEM((2, own_rows, units), F32),
            pltpu.VMEM((2, count, width), BF),
            pltpu.VMEM((2, count, units), BF),
            pltpu.VMEM((2, 4, own_rows, units), F32),
        ],
        compiler_params=pltpu.CompilerParams(vmem_limit_bytes=48 * MB),
    )(group, grad_final, symbols, char_pack, hh_full, live, embeds, *saved)


def per_device(
    tokens,
    char_ids,
    token_chars,
    groups,
    qkv_weight,
    out_weight,
    ffn_in,
    ffn_out,
    conv_weight,
    gains,
    ih_weight,
    hh_weight,
    gru_bias,
    char_table,
    group_table,
    token_cot,
    char_cot,
):
    dp_size, mp_size = lax.axis_size("dp"), lax.axis_size("mp")
    mp_index = lax.axis_index("mp")
    seq_len, model = tokens.shape
    local = out_weight.shape[0]
    head_size = model // HEADS
    heads = local // head_size
    own_rows = seq_len // mp_size

    def own_part(rows):
        return lax.dynamic_slice_in_dim(rows, mp_index * own_rows, own_rows, 0)

    qkv_full = gather_dp(jnp.transpose(qkv_weight, (1, 0, 2)), 1).reshape(3, model, local)

    ih_rows, ih_cols = ih_weight.shape
    symbols_n = char_table.shape[0]
    table_lanes = -(-symbols_n // 128) * 128
    vocab = jnp.pad(char_table.T, ((0, 0), (0, table_lanes - symbols_n)))
    group_count = group_table.shape[0]
    units = hh_weight.shape[1]
    bias_cols = gru_bias.shape[1]
    gain_cols = gains.shape[1]
    if quick():
        head = jnp.concatenate(
            [
                jnp.pad(gru_bias, ((0, 2), (0, GROUP_LANE - bias_cols))),
                jnp.pad(gains, ((0, 0), (0, GROUP_LANE - gain_cols))),
            ],
            0,
        )
    else:
        head = jnp.zeros((ih_rows, GROUP_LANE), BF)
    misc = jnp.concatenate(
        [head, group_table.T, jnp.zeros((ih_rows, 128 - GROUP_LANE - group_count), BF)], 1
    )
    char_pack4 = gather_all(jnp.concatenate([ih_weight, vocab, misc], 1))
    embed_dim = dp_size * mp_size * ih_rows
    char_pack = char_pack4.reshape(embed_dim, -1)
    misc_at = ih_cols + table_lanes
    if quick():
        small = char_pack4[:, :, :, misc_at:]
        bias_full = jnp.transpose(small[:, :, :2, :bias_cols], (2, 0, 1, 3)).reshape(2, -1)
        gain_full = jnp.transpose(small[:, 0, 4:, :gain_cols], (1, 0, 2)).reshape(4, -1)
    else:
        bias_full = lax.all_gather(gru_bias, ("dp", "mp"), axis=1, tiled=True)
        gain_full = lax.all_gather(gains, "dp", axis=1, tiled=True)
    bias_full = bias_full.astype(F32)
    gain_rows = gain_full.astype(F32)
    hh_full = gather_all(hh_weight).reshape(-1, units)

    out_full = gather_dp(gather_mp(out_weight.T), 1).reshape(mp_size, model, local)
    ffn_full = gather_dp(jnp.stack([ffn_in, ffn_out.T]), 1)
    in_full = ffn_full[0].reshape(model, -1)
    down_full = ffn_full[1].reshape(model, -1)
    conv_full = gather_dp(conv_weight).reshape(3, 2 * model, local)

    packed = [product(tokens, qkv_full[i]).astype(BF) for i in range(3)]
    queries, key_rows, values = [part.reshape(seq_len, heads, head_size) for part in packed]
    head_out, log_sum = attend_forward(queries, key_rows, values)
    attn_low = head_out.reshape(seq_len, local).astype(BF)
    attn_all = gather_mp(attn_low)
    first_sum = tokens.astype(F32)
    for part in range(mp_size):
        first_sum = first_sum + product_nt(attn_all[part], out_full[part])
    normal_one, _ = norm_parts(first_sum)
    normed_one = normal_one * gain_rows[0]
    normed_low = normed_one.astype(BF)
    hidden_pre = product(normed_low, in_full)
    hidden = gelu_fn(hidden_pre).astype(BF)
    down = product_nt(hidden, down_full).astype(BF)
    second = own_part(normed_one) + scatter_mp(down.reshape(mp_size, own_rows, model))
    normal_two, scale_two = norm_parts(second)
    normed_two = gather_mp((normal_two * gain_rows[1]).astype(BF)).reshape(seq_len, model)

    counts = token_chars[0]
    starts = jnp.cumsum(counts) - counts
    own_counts = own_part(counts)
    own_starts = own_part(starts)
    slots = jnp.arange(MAXC, dtype=jnp.int32)[:, None]
    ahead = own_starts[None, :] + jnp.minimum(slots, own_counts[None, :] - 1)
    behind = own_starts[None, :] + jnp.maximum(own_counts[None, :] - 1 - slots, 0)
    positions = jnp.stack([ahead, behind]).reshape(2, MAXC * own_rows, 1)
    spot = lax.broadcasted_iota(jnp.int32, (1, 1, char_ids.shape[1]), 2)
    symbols = jnp.sum(jnp.where(positions == spot, char_ids[0], 0), axis=-1, keepdims=True)
    live = (slots < own_counts[None, :]).astype(F32)[:, :, None]
    final, embeds, *saved = encoder_forward(
        symbols, groups, char_pack, hh_full, bias_full, live, table_lanes
    )
    char_rows = gather_mp(final).reshape(seq_len, model)

    mixed = jnp.concatenate([normed_two, char_rows], 1)
    earlier, later = rows_earlier(mixed), rows_later(mixed)
    joined_pre = (
        product(earlier, conv_full[0]) + product(mixed, conv_full[1]) + product(later, conv_full[2])
    )
    joined = gather_mp(gelu_fn(joined_pre).astype(BF))
    joined = jnp.concatenate([joined[i] for i in range(mp_size)], 1).astype(F32)
    token_sum = normed_two.astype(F32) + joined
    char_sum = char_rows.astype(F32) + joined
    normal_three, scale_three = norm_parts(token_sum)
    normal_four, scale_four = norm_parts(char_sum)
    token_out = (normal_three * gain_rows[2]).astype(BF)
    char_out = (normal_four * gain_rows[3]).astype(BF)

    grad_token_sum, gain_three = norm_back(
        normal_three, scale_three, gain_rows[2], token_cot.astype(F32)
    )
    grad_char_sum, gain_four = norm_back(
        normal_four, scale_four, gain_rows[3], char_cot.astype(F32)
    )
    share = 1.0 / mp_size
    grad_joined = lax.dynamic_slice_in_dim(
        grad_token_sum + grad_char_sum, mp_index * local, local, 1
    )
    grad_pre = (grad_joined * gelu_grad(joined_pre)).astype(BF)
    grad_mixed = (
        product_nt(grad_pre, conv_full[1])
        + rows_later(product_nt(grad_pre, conv_full[0]))
        + rows_earlier(product_nt(grad_pre, conv_full[2]))
    ).astype(BF)
    mixed_token = scatter_mp(grad_mixed[:, :model].reshape(mp_size, own_rows, model))
    mixed_char = scatter_mp(grad_mixed[:, model:].reshape(mp_size, own_rows, model))
    conv_grad = jnp.concatenate(
        [product_tn(part, grad_pre).astype(BF) for part in (earlier, mixed, later)], 0
    )
    conv_grad = scatter_dp(conv_grad.reshape(dp_size, -1, local))

    grad_second, gain_two = norm_back(
        normal_two, scale_two, gain_rows[1], own_part(grad_token_sum) + mixed_token
    )
    second_low = gather_mp(grad_second.astype(BF)).reshape(seq_len, model)
    grad_hidden = (product(second_low, down_full) * gelu_grad(hidden_pre)).astype(BF)
    grad_in = product_nt(grad_hidden, in_full).astype(BF)
    grad_normed_one = grad_second + scatter_mp(grad_in.reshape(mp_size, own_rows, model))
    down_grad = scatter_dp(product_tn(second_low, hidden).astype(BF).reshape(dp_size, -1, hidden.shape[1]))
    in_grad = scatter_dp(product_tn(normed_low, grad_hidden).astype(BF).reshape(dp_size, -1, hidden.shape[1]))

    own_normal, own_scale = norm_parts(own_part(first_sum))
    grad_first, gain_one = norm_back(own_normal, own_scale, gain_rows[0], grad_normed_one)
    first_low = gather_mp(grad_first.astype(BF)).reshape(seq_len, model)
    out_grad = scatter_dp(product_tn(first_low, attn_low).astype(BF).reshape(dp_size, -1, local))
    grad_attn = (
        product(first_low, take(out_full, mp_index)).astype(BF).reshape(seq_len, heads, head_size)
    )
    grad_packed = [
        part.reshape(seq_len, local).astype(BF)
        for part in attend_backward(queries, key_rows, values, log_sum, grad_attn)
    ]
    qkv_grad = jnp.stack([product_tn(tokens, part).astype(BF) for part in grad_packed], 0)
    qkv_grad = jnp.transpose(qkv_grad.reshape(3, dp_size, -1, local), (1, 0, 2, 3))
    qkv_grad = scatter_dp(qkv_grad)
    token_part = sum(product_nt(grad_packed[i], qkv_full[i]) for i in range(3)).astype(BF)
    token_own = grad_first + scatter_mp(token_part.reshape(mp_size, own_rows, model))
    token_grad = gather_mp(token_own.astype(BF)).reshape(seq_len, model).astype(F32)

    grad_final = own_part(grad_char_sum) + mixed_char
    pack_grad, hh_grad, bias_grad = encoder_backward(
        grad_final, symbols, groups, char_pack, hh_full, live, embeds, saved, table_lanes
    )
    bias_grad = bias_grad.reshape(2, -1)
    gain_grad = jnp.stack([gain_one, gain_two, gain_three * share, gain_four * share])
    if quick():
        bias_blocks = jnp.transpose(
            bias_grad.reshape(2, dp_size, mp_size, bias_cols), (1, 2, 0, 3)
        )
        pack4 = pack_grad.reshape(char_pack4.shape)
        hh4 = hh_grad.reshape((dp_size, mp_size) + hh_weight.shape)
        pack_own = scatter_mp(scatter_dp(pack4).astype(BF))
        hh_own = scatter_mp(scatter_dp(hh4).astype(BF))
        ih_grad = pack_own[:, :ih_cols]
        table_grad = pack_own[:, ih_cols : ih_cols + symbols_n].T
        group_at = misc_at + GROUP_LANE
        group_grad = pack_own[:, group_at : group_at + group_count].T
        gain_blocks = jnp.transpose(gain_grad.reshape(4, dp_size, gain_cols), (1, 0, 2))
        tail = jnp.concatenate(
            [
                jnp.pad(bias_blocks, ((0, 0), (0, 0), (0, 2), (0, 128 - bias_cols))),
                jnp.pad(
                    jnp.broadcast_to(
                        gain_blocks[:, None], (dp_size, mp_size) + gains.shape
                    ),
                    ((0, 0), (0, 0), (0, 0), (0, 128 - gain_cols)),
                ),
            ],
            2,
        )
        tail_own = scatter_mp(scatter_dp(tail.astype(BF)).astype(BF))
        bias_own = tail_own[:2, :bias_cols]
        gain_own = tail_own[4:, :gain_cols]
    else:
        both = ("dp", "mp")

        def spread(rows, axis):
            return lax.psum_scatter(
                rows.astype(F32), both, scatter_dimension=axis, tiled=True
            )

        table_at = ih_cols + symbols_n
        group_at = misc_at + GROUP_LANE
        ih_grad = spread(pack_grad[:, :ih_cols], 0)
        hh_own = spread(hh_grad, 0)
        table_grad = spread(pack_grad[:, ih_cols:table_at].T, 1)
        group_grad = spread(pack_grad[:, group_at : group_at + group_count].T, 1)
        bias_own = spread(bias_grad, 1)
        gain_own = lax.psum_scatter(
            lax.psum(gain_grad, "mp"), "dp", scatter_dimension=1, tiled=True
        )
    return (
        token_out,
        char_out,
        token_grad,
        jnp.transpose(qkv_grad, (1, 0, 2)),
        out_grad.T,
        in_grad,
        down_grad.T,
        conv_grad,
        gain_own,
        ih_grad,
        hh_own,
        bias_own,
        table_grad,
        group_grad,
    )


def solution(mesh):
    return jax.shard_map(
        per_device,
        mesh=mesh,
        in_specs=(
            P("dp", None),
            P("dp", None),
            P("dp", None),
            P("dp"),
            P("dp", None, "mp"),
            P("mp", "dp"),
            P("dp", "mp"),
            P("mp", "dp"),
            P("dp", "mp"),
            P(None, "dp"),
            P(("dp", "mp"), None),
            P(("dp", "mp"), None),
            P(None, ("dp", "mp")),
            P(None, ("dp", "mp")),
            P(None, ("dp", "mp")),
            P("dp", None),
            P("dp", None),
        ),
        out_specs=(
            P("dp", None),
            P("dp", None),
            P("dp", None),
            P("dp", None, "mp"),
            P("mp", "dp"),
            P("dp", "mp"),
            P("mp", "dp"),
            P("dp", "mp"),
            P(None, "dp"),
            P(("dp", "mp"), None),
            P(("dp", "mp"), None),
            P(None, ("dp", "mp")),
            P(None, ("dp", "mp")),
            P(None, ("dp", "mp")),
        ),
        check_vma=False,
    )
```

time: 1370 us -> 479 us (0.35)
  waiting for transfers between devices: 698 us -> 126 us
  blocking collectives: 356 us -> 0 us
  starting transfers between devices: 1.64 us -> 146 us
  matrix products: 87.8 us -> 33.1 us
  Pallas kernels: 0 us -> 50.1 us
  other arithmetic: 95.6 us -> 45.7 us
  local copies, waits for them, and re-layouts: 105 us -> 70.5 us
  between operations: 21.1 us -> 3.6 us
    unnamed x31 -> x0, waiting for transfers between devices: 346 us -> none
    all_gather x11 -> x0, blocking collectives: 316 us -> none  [the longest x1 73.4 us: per_device(): lax.all_gather(char_table, ('dp', 'mp'), axis=1, tiled=True)]
    reduce_scatter x4 -> x0, waiting for transfers between devices: 240 us -> none  [the longest x1 101 us: per_device(): lax.psum_scatter(ih_grad, ('dp', 'mp'), scatter_dimension=0, tiled=True)]
    ppermute x0 -> x128, starting transfers between devices: none -> 146 us  [swap(): return lax.ppermute(rows, axis, [(i, i ^ mask) for i in range(size)])]
    ppermute x0 -> x128, waiting for transfers between devices: none -> 126 us  [swap(): return lax.ppermute(rows, axis, [(i, i ^ mask) for i in range(size)])]
    psum x5 -> x0, waiting for transfers between devices: 81.3 us -> none  [the longest x1 52.9 us: per_device(): lax.psum(grad_mixed_part.astype(jnp.bfloat16), 'mp').astype(jnp.float32)]
    dot_general x76 -> x34, matrix products: 85.6 us -> 31.7 us  [the longest x30 29.8 us: dot(): lax.dot_general(left, right, (dims, ((), ())), preferred_element_type=F32)]
    pallas_call x0 -> x18, Pallas kernels: none -> 50.1 us  [the longest x16 24.7 us: place(): pl.pallas_call(body, out_shape=jax.ShapeDtypeStruct(shape, first.dtype),...]
  transfers between devices with their start and end apart: 25 -> 128, of which waited for: 14 -> 45; matrix products, arithmetic and copies ran while one was open for 15% -> 18% of each run, Pallas kernels for 0% -> 10%
where the time goes in v1:
time: 479 us; the launch traced here: 474 us
  starting transfers between devices  146 us (30%)
  waiting for transfers between devices  126 us (26%)
  local copies, waits for them, and re-layouts  70.5 us (15%)
  Pallas kernels  50.1 us (10%)
  other arithmetic  45.7 us (10%)
  matrix products  33.1 us (7%)
    ppermute x128, starting transfers between devices, swap(): return lax.ppermute(rows, axis, [(i, i ^ mask) for i in range(size)])  146 us
    ppermute x128, waiting for transfers between devices, swap(): return lax.ppermute(rows, axis, [(i, i ^ mask) for i in range(size)])  126 us
    dot_general x30, matrix products, dot(): lax.dot_general(left, right, (dims, ((), ())), preferred_element_type=F32)  29.8 us
    pallas_call x16, Pallas kernels, place(): pl.pallas_call(body, out_shape=jax.ShapeDtypeStruct(shape, first.dtype),...  24.7 us
    unnamed x247, local copies, waits for them, and re-layouts  23 us
    pallas_call x1, Pallas kernels, encoder_backward(): pl.pallas_call(body, out_shape=[jax.ShapeDtypeStruct(char_pack.shape, BF)...  16.5 us
    dynamic_slice x5, local copies, waits for them, and re-layouts, take(): return lax.dynamic_index_in_dim(blocks, index, axis, keepdims=False)  10.4 us
  transfers between devices with their start and end apart: 128, of which 45 were waited for; matrix products, arithmetic and copies ran while one was open for 18% of the time, Pallas kernels for 10%

profile of v1, /device:TPU:0, one launch (start us, length us, event | category | flops | bytes accessed | tf_op | source)
XLA Modules:
  0.0 474.3 jit_solution(11208844063753516492)
XLA Ops:
  1.6 5.1 %collective-permute-start.12 = (bf16[96,192]{1,0:T(8,128)(2,1)S(1)}, bf16[96,192]{1,0:T(8,128)(2,1)S(1)}, u32[]{:S(2)}, u32[]{:S(2)}) collective-permute-start(bf16[96,192]{1,0:T(8,128)(2,1)S(1)} %bitcast.445), channel_id=1, source_target_pairs={{0,3},{1,2},{2,1},{3,0},{4,7},{5,6},{6,5},{7,4},{8,11},{9,10},{10,... | collective-permute-start | bytes 110600 | tf_op jit(solution)/shard_map/ppermute | solution.py:35
  9.6 3.7 collective-permute-start.22
  37.1 2.7 collective-permute-done.15.refs_3_
  52.3 3.7 collective-permute-start.9
  63.6 7.9 %collective-permute-done.8.refs_2_ = bf16[384,192]{1,0:T(8,128)(2,1)S(1)} collective-permute-done((bf16[384,192]{1,0:T(8,128)(2,1)S(1)}, bf16[384,192]{1,0:T(8,128)(2,1)S(1)}, u32[]{:S(2)}, u32[]{:S(2)}) %collective-permute-start.8) | collective-permute-done | bytes 147488 | tf_op jit(solution)/shard_map/ppermute | solution.py:35
  83.9 2.9 shard_map.277
  86.8 6.0 %collective-permute-done.48.refs_3_ = bf16[4,72,384]{2,1,0:T(8,128)(2,1)S(1)} collective-permute-done((bf16[4,72,384]{2,1,0:T(8,128)(2,1)S(1)}, bf16[4,72,384]{2,1,0:T(8,128)(2,1)S(1)}, u32[]{:S(2)}, u32[]{:S(2)}) %collective-permute-start.48) | collective-permute-done | bytes 221216 | tf_op jit(solution)/shard_map/ppermute | solution.py:35
  98.4 5.0 %collective-permute-done.46.refs_1_ = bf16[4,72,384]{2,1,0:T(8,128)(2,1)S(1)} collective-permute-done((bf16[4,72,384]{2,1,0:T(8,128)(2,1)S(1)}, bf16[4,72,384]{2,1,0:T(8,128)(2,1)S(1)}, u32[]{:S(2)}, u32[]{:S(2)}) %collective-permute-start.46) | collective-permute-done | bytes 221216 | tf_op jit(solution)/shard_map/ppermute | solution.py:35
  130.7 9.0 %shard_map.282 = (bf16[96,768]{1,0:T(8,128)(2,1)S(1)}, bf16[2,8,96,256]{3,2,1,0:T(8,128)(2,1)S(1)}, bf16[2,8,96,384]{3,2,1,0:T(8,128)(2,1)S(1)}, bf16[2,8,96,384...) custom-call(s32[1]{0:T(128)S(6)} %copy.194.group_ref, ...), custom_call_target="tpu_custom_call" | custom-call | tf_op jit(solution)/shard_map/pallas_call | solution.py:246
  149.9 5.0 %collective-permute-start.40 = (bf16[96,768]{1,0:T(8,128)(2,1)S(1)}, bf16[96,768]{1,0:T(8,128)(2,1)S(1)}, u32[]{:S(2)}, u32[]{:S(2)}) collective-permute-start(bf16[96,768]{1,0:T(8,128)(2,1)S(1)} %multiply_convert_fusion.5.refs_0_), channel_id=1, source_target_pairs={{0,1},{1,0},{2,3},{3,2},{4,5},{5,4},{6,7},{7,6},{8,9},{9,8},{10,11... | collective-permute-start | bytes 442376 | tf_op jit(solution)/shard_map/ppermute | solution.py:35
  158.0 5.8 %collective-permute-done.54.refs_2_ = bf16[96,768]{1,0:T(8,128)(2,1)S(1)} collective-permute-done((bf16[96,768]{1,0:T(8,128)(2,1)S(1)}, bf16[96,768]{1,0:T(8,128)(2,1)S(1)}, u32[]{:S(2)}, u32[]{:S(2)}) %collective-permute-start.54) | collective-permute-done | bytes 147488 | tf_op jit(solution)/shard_map/ppermute | solution.py:35
  165.1 4.1 collective-permute-done.41.refs_2_
  179.5 4.3 collective-permute-done.65.refs_3_
  183.8 7.9 %collective-permute-done.64.refs_2_ = bf16[384,192]{1,0:T(8,128)(2,1)} collective-permute-done((bf16[384,192]{1,0:T(8,128)(2,1)}, bf16[384,192]{1,0:T(8,128)(2,1)}, u32[]{:S(2)}, u32[]{:S(2)}) %collective-permute-start.64) | collective-permute-done | bytes 147488 | tf_op jit(solution)/shard_map/ppermute | solution.py:35
  197.8 2.7 multiply_reduce_fusion.1
  207.1 3.9 fusion.30
  222.6 6.3 %reshape_reshape.25 = bf16[4,2,576,192]{2,1,0,3:T(2,128)(2,1)} reshape(bf16[4608,192]{0,1:T(8,128)(2,1)} %pad_maximum_fusion) | data formatting | bytes 3538944 | tf_op jit(solution)/shard_map/reshape;reshape | solution.py:116
  229.0 3.0 fusion.1
  237.2 5.3 %constant_dynamic-slice_fusion.9 = (bf16[4,1,576,192]{2,1,0,3:T(2,128)(2,1)S(1)}, bf16[4,1,576,192]{2,1,0,3:T(2,128)(2,1)}) fusion(bf16[4,2,576,192]{2,1,0,3:T(2,128)(2,1)S(1)} %copy-done.46, s32[]{:T(128)S(6)} %select_n.141, s32[]{:T(128)S(6)} %select_n.142), kind=kLoop, calls=%fused_computation.288 | loop fusion | bytes 3538952 | tf_op jit(solution)/shard_map/jit(dynamic_index_in_dim)/dynamic_slice | solution.py:100
  242.7 2.8 copy.187
  255.9 11.0 %collective-permute-start.69 = (bf16[96,768]{1,0:T(8,128)(2,1)S(1)}, bf16[96,768]{1,0:T(8,128)(2,1)S(1)}, u32[]{:S(2)}, u32[]{:S(2)}) collective-permute-start(bf16[96,768]{1,0:T(8,128)(2,1)S(1)} %get-tuple-element.57.refs_0_), channel_id=1, source_target_pairs={{0,1},{1,0},{2,3},{3,2},{4,5},{5,4},{6,7},{7,6},{8,9},{9,8},{10,11... | collective-permute-start | bytes 442376 | tf_op jit(solution)/shard_map/ppermute | solution.py:35
  270.7 16.5 %shard_map.289 = (bf16[256,3456]{1,0:T(8,128)(2,1)}, bf16[2304,384]{1,0:T(8,128)(2,1)}, f32[2,4,384]{2,1,0:T(4,128)S(1)}) custom-call(s32[1]{0:T(128)S(6)} %copy.194.group_ref, f32[96,768]{1,0:T(8,128)S(1)} %fusion.78.grad_in, s32[2,768,1]{2,1,0:T(8,128)S(1)} %copy-done.4, bf16[256,3456]{1,0:T(8,128)(2,1)} %bitcast.425, bf16[2304,384]{1,0:T(8,128)(2,1)} %bitcast.427, ...), custom_call_target="tpu_custom_call" | custom-call | tf_op jit(solution)/shard_map/pallas_call | solution.py:329
  308.2 5.8 %collective-permute-done.73 = bf16[96,768]{1,0:T(8,128)(2,1)S(1)} collective-permute-done((bf16[96,768]{1,0:T(8,128)(2,1)S(1)}, bf16[96,768]{1,0:T(8,128)(2,1)S(1)}, u32[]{:S(2)}, u32[]{:S(2)}) %collective-permute-start.73) | collective-permute-done | bytes 147488 | tf_op jit(solution)/shard_map/ppermute | solution.py:35
  334.1 3.0 collective-permute-done.77.refs_3_
  337.2 5.3 %collective-permute-done.76.refs_2_ = bf16[96,768]{1,0:T(8,128)(2,1)S(1)} collective-permute-done((bf16[96,768]{1,0:T(8,128)(2,1)S(1)}, bf16[96,768]{1,0:T(8,128)(2,1)S(1)}, u32[]{:S(2)}, u32[]{:S(2)}) %collective-permute-start.76) | collective-permute-done | bytes 147488 | tf_op jit(solution)/shard_map/ppermute | solution.py:35
  373.4 3.2 collective-permute-done.80
  377.5 6.2 %collective-permute-done.79 = bf16[96,768]{1,0:T(8,128)(2,1)S(1)} collective-permute-done((bf16[96,768]{1,0:T(8,128)(2,1)S(1)}, bf16[96,768]{1,0:T(8,128)(2,1)S(1)}, u32[]{:S(2)}, u32[]{:S(2)}) %collective-permute-start.79) | collective-permute-done | bytes 147488 | tf_op jit(solution)/shard_map/ppermute | solution.py:35
  384.8 3.0 collective-permute-done.90
  397.0 6.2 %collective-permute-done.82.refs_2_ = bf16[96,768]{1,0:T(8,128)(2,1)S(1)} collective-permute-done((bf16[96,768]{1,0:T(8,128)(2,1)S(1)}, bf16[96,768]{1,0:T(8,128)(2,1)S(1)}, u32[]{:S(2)}, u32[]{:S(2)}) %collective-permute-start.82) | collective-permute-done | bytes 147488 | tf_op jit(solution)/shard_map/ppermute | solution.py:35
  412.3 8.2 %collective-permute-done.93 = bf16[96,768]{1,0:T(8,128)(2,1)S(1)} collective-permute-done((bf16[96,768]{1,0:T(8,128)(2,1)S(1)}, bf16[96,768]{1,0:T(8,128)(2,1)S(1)}, u32[]{:S(2)}, u32[]{:S(2)}) %collective-permute-start.93) | collective-permute-done | bytes 147488 | tf_op jit(solution)/shard_map/ppermute | solution.py:35
  435.8 2.9 collective-permute-start.85
  457.2 4.2 collective-permute-done.116
  (684 shorter events, 297.8 us)
Async XLA Ops:
  1.6 15.0 %collective-permute-start.12 = (bf16[96,192]{1,0:T(8,128)(2,1)S(1)}, bf16[96,192]{1,0:T(8,128)(2,1)S(1)}, u32[]{:S(2)}, u32[]{:S(2)}) collective-permute-start(bf16[96,192]{1,0:T(8,128)(2,1)S(1)} %bitcast.445), channel_id=1, source_target_pairs={{0,3},{1,2},{2,1},{3,0},{4,7},{5,6},{6,5},{7,4},{8,11},{9,10},{10,... | collective-permute-start | bytes 110600 | tf_op jit(solution)/shard_map/ppermute | solution.py:35
  42.2 50.7 %collective-permute-start.32 = (bf16[2,96,768]{2,1,0:T(8,128)(2,1)S(1)}, bf16[2,96,768]{2,1,0:T(8,128)(2,1)S(1)}, u32[]{:S(2)}, u32[]{:S(2)}) collective-permute-start(bf16[2,96,768]{2,1,0:T(8,128)(2,1)S(1)} %pad_maximum_fusion.7.refs_0_), channel_id=1, source_target_pairs={{0,24},{4,28},{8,16},{12,20},{16,8},{20,12},{24,0},{28,4},{1,25},{... | collective-permute-start | bytes 884744 | tf_op jit(solution)/shard_map/ppermute | solution.py:35
  56.0 15.5 %collective-permute-start.8 = (bf16[384,192]{1,0:T(8,128)(2,1)S(1)}, bf16[384,192]{1,0:T(8,128)(2,1)S(1)}, u32[]{:S(2)}, u32[]{:S(2)}) collective-permute-start(bf16[384,192]{1,0:T(8,128)(2,1)S(1)} %copy.125.refs_0_), channel_id=1, source_target_pairs={{0,2},{1,3},{2,0},{3,1},{4,6},{5,7},{6,4},{7,5},{8,10},{9,11},{10,... | collective-permute-start | bytes 442376 | tf_op jit(solution)/shard_map/ppermute | solution.py:35
  56.0 17.0 %collective-permute-start.7 = (bf16[384,192]{1,0:T(8,128)(2,1)S(1)}, bf16[384,192]{1,0:T(8,128)(2,1)S(1)}, u32[]{:S(2)}, u32[]{:S(2)}) collective-permute-start(bf16[384,192]{1,0:T(8,128)(2,1)S(1)} %copy.125.refs_0_), channel_id=1, source_target_pairs={{0,1},{1,0},{2,3},{3,2},{4,5},{5,4},{6,7},{7,6},{8,9},{9,8},{10,11... | collective-permute-start | bytes 442376 | tf_op jit(solution)/shard_map/ppermute | solution.py:35
  60.3 17.1 %collective-permute-start.26 = (bf16[4,8,3456]{2,1,0:T(8,128)(2,1)S(1)}, bf16[4,8,3456]{2,1,0:T(8,128)(2,1)S(1)}, u32[]{:S(2)}, u32[]{:S(2)}) collective-permute-start(bf16[4,8,3456]{2,1,0:T(8,128)(2,1)S(1)} %shard_map.276.refs_0_), channel_id=1, source_target_pairs={{0,4},{4,0},{8,12},{12,8},{16,20},{20,16},{24,28},{28,24},{1,5},{5... | collective-permute-start | bytes 663560 | tf_op jit(solution)/shard_map/ppermute | solution.py:35
  62.0 16.9 %collective-permute-start.24 = (bf16[4,8,3456]{2,1,0:T(8,128)(2,1)S(1)}, bf16[4,8,3456]{2,1,0:T(8,128)(2,1)S(1)}, u32[]{:S(2)}, u32[]{:S(2)}) collective-permute-start(bf16[4,8,3456]{2,1,0:T(8,128)(2,1)S(1)} %shard_map.276.refs_0_), channel_id=1, source_target_pairs={{0,16},{4,20},{8,24},{12,28},{16,0},{20,4},{24,8},{28,12},{1,17},{... | collective-permute-start | bytes 663560 | tf_op jit(solution)/shard_map/ppermute | solution.py:35
  77.3 16.0 %collective-permute-start.31 = (bf16[2,96,768]{2,1,0:T(8,128)(2,1)S(1)}, bf16[2,96,768]{2,1,0:T(8,128)(2,1)S(1)}, u32[]{:S(2)}, u32[]{:S(2)}) collective-permute-start(bf16[2,96,768]{2,1,0:T(8,128)(2,1)S(1)} %pad_maximum_fusion.7.refs_0_), channel_id=1, source_target_pairs={{0,16},{4,20},{8,24},{12,28},{16,0},{20,4},{24,8},{28,12},{1,17},{... | collective-permute-start | bytes 884744 | tf_op jit(solution)/shard_map/ppermute | solution.py:35
  112.3 27.5 %collective-permute-start.57 = (bf16[576,192]{1,0:T(8,128)(2,1)}, bf16[576,192]{1,0:T(8,128)(2,1)}, u32[]{:S(2)}, u32[]{:S(2)}) collective-permute-start(bf16[576,192]{1,0:T(8,128)(2,1)} %copy.133.refs_0_), channel_id=1, source_target_pairs={{0,16},{4,20},{8,24},{12,28},{16,0},{20,4},{24,8},{28,12},{1,17},{... | collective-permute-start | bytes 663560 | tf_op jit(solution)/shard_map/ppermute | solution.py:35
  114.6 25.3 %collective-permute-start.56 = (bf16[576,192]{1,0:T(8,128)(2,1)}, bf16[576,192]{1,0:T(8,128)(2,1)}, u32[]{:S(2)}, u32[]{:S(2)}) collective-permute-start(bf16[576,192]{1,0:T(8,128)(2,1)} %copy.133.refs_0_), channel_id=1, source_target_pairs={{0,8},{4,12},{8,0},{12,4},{16,24},{20,28},{24,16},{28,20},{1,9},{5... | collective-permute-start | bytes 663560 | tf_op jit(solution)/shard_map/ppermute | solution.py:35
  115.8 24.6 %collective-permute-start.37 = (bf16[96,768]{1,0:T(8,128)(2,1)}, bf16[96,768]{1,0:T(8,128)(2,1)}, u32[]{:S(2)}, u32[]{:S(2)}) collective-permute-start(bf16[96,768]{1,0:T(8,128)(2,1)} %get-tuple-element.125), channel_id=1, source_target_pairs={{0,1},{1,0},{2,3},{3,2},{4,5},{5,4},{6,7},{7,6},{8,9},{9,8},{10,11... | collective-permute-start | bytes 442376 | tf_op jit(solution)/shard_map/ppermute | solution.py:35
  116.5 24.0 %collective-permute-start.39 = (bf16[96,768]{1,0:T(8,128)(2,1)}, bf16[96,768]{1,0:T(8,128)(2,1)}, u32[]{:S(2)}, u32[]{:S(2)}) collective-permute-start(bf16[96,768]{1,0:T(8,128)(2,1)} %get-tuple-element.126), channel_id=1, source_target_pairs={{0,3},{1,2},{2,1},{3,0},{4,7},{5,6},{6,5},{7,4},{8,11},{9,10},{10,... | collective-permute-start | bytes 442376 | tf_op jit(solution)/shard_map/ppermute | solution.py:35
  119.5 21.4 %collective-permute-start.38 = (bf16[96,768]{1,0:T(8,128)(2,1)}, bf16[96,768]{1,0:T(8,128)(2,1)}, u32[]{:S(2)}, u32[]{:S(2)}) collective-permute-start(bf16[96,768]{1,0:T(8,128)(2,1)} %get-tuple-element.127), channel_id=1, source_target_pairs={{0,2},{1,3},{2,0},{3,1},{4,6},{5,7},{6,4},{7,5},{8,10},{9,11},{10,... | collective-permute-start | bytes 442376 | tf_op jit(solution)/shard_map/ppermute | solution.py:35
  145.4 18.3 %collective-permute-start.54 = (bf16[96,768]{1,0:T(8,128)(2,1)S(1)}, bf16[96,768]{1,0:T(8,128)(2,1)S(1)}, u32[]{:S(2)}, u32[]{:S(2)}) collective-permute-start(bf16[96,768]{1,0:T(8,128)(2,1)S(1)} %get-tuple-element.24.refs_0_), channel_id=1, source_target_pairs={{0,2},{1,3},{2,0},{3,1},{4,6},{5,7},{6,4},{7,5},{8,10},{9,11},{10,... | collective-permute-start | bytes 442376 | tf_op jit(solution)/shard_map/ppermute | solution.py:35
  145.9 17.8 %collective-permute-start.53 = (bf16[96,768]{1,0:T(8,128)(2,1)S(1)}, bf16[96,768]{1,0:T(8,128)(2,1)S(1)}, u32[]{:S(2)}, u32[]{:S(2)}) collective-permute-start(bf16[96,768]{1,0:T(8,128)(2,1)S(1)} %get-tuple-element.24.refs_0_), channel_id=1, source_target_pairs={{0,1},{1,0},{2,3},{3,2},{4,5},{5,4},{6,7},{7,6},{8,9},{9,8},{10,11... | collective-permute-start | bytes 442376 | tf_op jit(solution)/shard_map/ppermute | solution.py:35
  147.5 17.6 %collective-permute-start.42 = (bf16[96,768]{1,0:T(8,128)(2,1)S(1)}, bf16[96,768]{1,0:T(8,128)(2,1)S(1)}, u32[]{:S(2)}, u32[]{:S(2)}) collective-permute-start(bf16[96,768]{1,0:T(8,128)(2,1)S(1)} %multiply_convert_fusion.5.refs_0_), channel_id=1, source_target_pairs={{0,3},{1,2},{2,1},{3,0},{4,7},{5,6},{6,5},{7,4},{8,11},{9,10},{10,... | collective-permute-start | bytes 442376 | tf_op jit(solution)/shard_map/ppermute | solution.py:35
  149.9 19.3 %collective-permute-start.41 = (bf16[96,768]{1,0:T(8,128)(2,1)S(1)}, bf16[96,768]{1,0:T(8,128)(2,1)S(1)}, u32[]{:S(2)}, u32[]{:S(2)}) collective-permute-start(bf16[96,768]{1,0:T(8,128)(2,1)S(1)} %multiply_convert_fusion.5.refs_0_), channel_id=1, source_target_pairs={{0,2},{1,3},{2,0},{3,1},{4,6},{5,7},{6,4},{7,5},{8,10},{9,11},{10,... | collective-permute-start | bytes 442376 | tf_op jit(solution)/shard_map/ppermute | solution.py:35
  149.9 19.3 %collective-permute-start.40 = (bf16[96,768]{1,0:T(8,128)(2,1)S(1)}, bf16[96,768]{1,0:T(8,128)(2,1)S(1)}, u32[]{:S(2)}, u32[]{:S(2)}) collective-permute-start(bf16[96,768]{1,0:T(8,128)(2,1)S(1)} %multiply_convert_fusion.5.refs_0_), channel_id=1, source_target_pairs={{0,1},{1,0},{2,3},{3,2},{4,5},{5,4},{6,7},{7,6},{8,9},{9,8},{10,11... | collective-permute-start | bytes 442376 | tf_op jit(solution)/shard_map/ppermute | solution.py:35
  176.1 15.6 %collective-permute-start.64 = (bf16[384,192]{1,0:T(8,128)(2,1)}, bf16[384,192]{1,0:T(8,128)(2,1)}, u32[]{:S(2)}, u32[]{:S(2)}) collective-permute-start(bf16[384,192]{1,0:T(8,128)(2,1)} %get-tuple-element.156.refs_0_), channel_id=1, source_target_pairs={{0,2},{1,3},{2,0},{3,1},{4,6},{5,7},{6,4},{7,5},{8,10},{9,11},{10,... | collective-permute-start | bytes 442376 | tf_op jit(solution)/shard_map/ppermute | solution.py:35
  176.1 15.6 %collective-permute-start.63 = (bf16[384,192]{1,0:T(8,128)(2,1)}, bf16[384,192]{1,0:T(8,128)(2,1)}, u32[]{:S(2)}, u32[]{:S(2)}) collective-permute-start(bf16[384,192]{1,0:T(8,128)(2,1)} %get-tuple-element.156.refs_0_), channel_id=1, source_target_pairs={{0,1},{1,0},{2,3},{3,2},{4,5},{5,4},{6,7},{7,6},{8,9},{9,8},{10,11... | collective-permute-start | bytes 442376 | tf_op jit(solution)/shard_map/ppermute | solution.py:35
  245.5 145.9 %collective-permute-start.100 = (bf16[4,576,192]{1,2,0:T(8,128)(2,1)}, bf16[4,576,192]{1,2,0:T(8,128)(2,1)}, u32[]{:S(2)}, u32[]{:S(2)}) collective-permute-start(bf16[4,576,192]{1,2,0:T(8,128)(2,1)} %bitcast.417), channel_id=1, source_target_pairs={{0,4},{4,0},{8,12},{12,8},{16,20},{20,16},{24,28},{28,24},{1,5},{5... | collective-permute-start | bytes 2654216 | tf_op jit(solution)/shard_map/ppermute | solution.py:35
  248.0 21.6 %collective-permute-start.105 = (bf16[96,768]{1,0:T(8,128)(2,1)S(1)}, bf16[96,768]{1,0:T(8,128)(2,1)S(1)}, u32[]{:S(2)}, u32[]{:S(2)}) collective-permute-start(bf16[96,768]{1,0:T(8,128)(2,1)S(1)} %get-tuple-element.106), channel_id=1, source_target_pairs={{0,2},{1,3},{2,0},{3,1},{4,6},{5,7},{6,4},{7,5},{8,10},{9,11},{10,... | collective-permute-start | bytes 442376 | tf_op jit(solution)/shard_map/ppermute | solution.py:35
  251.8 40.8 %collective-permute-start.71 = (bf16[96,768]{1,0:T(8,128)(2,1)S(1)}, bf16[96,768]{1,0:T(8,128)(2,1)S(1)}, u32[]{:S(2)}, u32[]{:S(2)}) collective-permute-start(bf16[96,768]{1,0:T(8,128)(2,1)S(1)} %get-tuple-element.57.refs_0_), channel_id=1, source_target_pairs={{0,3},{1,2},{2,1},{3,0},{4,7},{5,6},{6,5},{7,4},{8,11},{9,10},{10,... | collective-permute-start | bytes 442376 | tf_op jit(solution)/shard_map/ppermute | solution.py:35
  255.5 37.1 %collective-permute-start.70 = (bf16[96,768]{1,0:T(8,128)(2,1)S(1)}, bf16[96,768]{1,0:T(8,128)(2,1)S(1)}, u32[]{:S(2)}, u32[]{:S(2)}) collective-permute-start(bf16[96,768]{1,0:T(8,128)(2,1)S(1)} %get-tuple-element.57.refs_0_), channel_id=1, source_target_pairs={{0,2},{1,3},{2,0},{3,1},{4,6},{5,7},{6,4},{7,5},{8,10},{9,11},{10,... | collective-permute-start | bytes 442376 | tf_op jit(solution)/shard_map/ppermute | solution.py:35
  255.9 36.6 %collective-permute-start.69 = (bf16[96,768]{1,0:T(8,128)(2,1)S(1)}, bf16[96,768]{1,0:T(8,128)(2,1)S(1)}, u32[]{:S(2)}, u32[]{:S(2)}) collective-permute-start(bf16[96,768]{1,0:T(8,128)(2,1)S(1)} %get-tuple-element.57.refs_0_), channel_id=1, source_target_pairs={{0,1},{1,0},{2,3},{3,2},{4,5},{5,4},{6,7},{7,6},{8,9},{9,8},{10,11... | collective-permute-start | bytes 442376 | tf_op jit(solution)/shard_map/ppermute | solution.py:35
  303.3 85.1 %collective-permute-start.92 = (bf16[4,96,768]{2,1,0:T(8,128)(2,1)}, bf16[4,96,768]{2,1,0:T(8,128)(2,1)}, u32[]{:S(2)}, u32[]{:S(2)}) collective-permute-start(bf16[4,96,768]{2,1,0:T(8,128)(2,1)} %dynamic-slice_bitcast_fusion.3), channel_id=1, source_target_pairs={{0,4},{4,0},{8,12},{12,8},{16,20},{20,16},{24,28},{28,24},{1,5},{5... | collective-permute-start | bytes 1769480 | tf_op jit(solution)/shard_map/ppermute | solution.py:35
  369.0 14.7 %collective-permute-start.79 = (bf16[96,768]{1,0:T(8,128)(2,1)S(1)}, bf16[96,768]{1,0:T(8,128)(2,1)S(1)}, u32[]{:S(2)}, u32[]{:S(2)}) collective-permute-start(bf16[96,768]{1,0:T(8,128)(2,1)S(1)} %get-tuple-element.118), channel_id=1, source_target_pairs={{0,2},{1,3},{2,0},{3,1},{4,6},{5,7},{6,4},{7,5},{8,10},{9,11},{10,... | collective-permute-start | bytes 442376 | tf_op jit(solution)/shard_map/ppermute | solution.py:35
  384.2 23.4 %collective-permute-start.121 = (bf16[4,4,72,384]{3,2,1,0:T(8,128)(2,1)S(1)}, bf16[4,4,72,384]{3,2,1,0:T(8,128)(2,1)S(1)}, u32[]{:S(2)}, u32[]{:S(2)}) collective-permute-start(bf16[4,4,72,384]{3,2,1,0:T(8,128)(2,1)S(1)} %copy-done.94), channel_id=1, source_target_pairs={{0,4},{4,0},{8,12},{12,8},{16,20},{20,16},{24,28},{28,24},{1,5},{5... | collective-permute-start | bytes 2654216 | tf_op jit(solution)/shard_map/ppermute | solution.py:35
  384.3 25.2 %collective-permute-start.114 = (bf16[4,4,8,3456]{3,2,1,0:T(8,128)(2,1)S(1)}, bf16[4,4,8,3456]{3,2,1,0:T(8,128)(2,1)S(1)}, u32[]{:S(2)}, u32[]{:S(2)}) collective-permute-start(bf16[4,4,8,3456]{3,2,1,0:T(8,128)(2,1)S(1)} %copy-done.93), channel_id=1, source_target_pairs={{0,4},{4,0},{8,12},{12,8},{16,20},{20,16},{24,28},{28,24},{1,5},{5... | collective-permute-start | bytes 2654216 | tf_op jit(solution)/shard_map/ppermute | solution.py:35
  403.2 32.6 %collective-permute-start.101 = (bf16[576,192]{0,1:T(8,128)(2,1)S(1)}, bf16[576,192]{0,1:T(8,128)(2,1)S(1)}, u32[]{:S(2)}, u32[]{:S(2)}) collective-permute-start(bf16[576,192]{0,1:T(8,128)(2,1)S(1)} %get-tuple-element.83), channel_id=1, source_target_pairs={{0,8},{4,12},{8,0},{12,4},{16,24},{20,28},{24,16},{28,20},{1,9},{5... | collective-permute-start | bytes 663560 | tf_op jit(solution)/shard_map/ppermute | solution.py:35
  403.7 35.1 %collective-permute-start.103 = (bf16[576,192]{0,1:T(8,128)(2,1)S(1)}, bf16[576,192]{0,1:T(8,128)(2,1)S(1)}, u32[]{:S(2)}, u32[]{:S(2)}) collective-permute-start(bf16[576,192]{0,1:T(8,128)(2,1)S(1)} %get-tuple-element.84), channel_id=1, source_target_pairs={{0,24},{4,28},{8,16},{12,20},{16,8},{20,12},{24,0},{28,4},{1,25},{... | collective-permute-start | bytes 663560 | tf_op jit(solution)/shard_map/ppermute | solution.py:35
  429.7 33.4 %collective-permute-start.122 = (bf16[4,72,384]{2,1,0:T(8,128)(2,1)S(1)}, bf16[4,72,384]{2,1,0:T(8,128)(2,1)S(1)}, u32[]{:S(2)}, u32[]{:S(2)}) collective-permute-start(bf16[4,72,384]{2,1,0:T(8,128)(2,1)S(1)} %get-tuple-element.86), channel_id=1, source_target_pairs={{0,8},{4,12},{8,0},{12,4},{16,24},{20,28},{24,16},{28,20},{1,9},{5... | collective-permute-start | bytes 663560 | tf_op jit(solution)/shard_map/ppermute | solution.py:35
  433.5 31.6 %collective-permute-start.124 = (bf16[4,72,384]{2,1,0:T(8,128)(2,1)S(1)}, bf16[4,72,384]{2,1,0:T(8,128)(2,1)S(1)}, u32[]{:S(2)}, u32[]{:S(2)}) collective-permute-start(bf16[4,72,384]{2,1,0:T(8,128)(2,1)S(1)} %get-tuple-element.87), channel_id=1, source_target_pairs={{0,24},{4,28},{8,16},{12,20},{16,8},{20,12},{24,0},{28,4},{1,25},{... | collective-permute-start | bytes 663560 | tf_op jit(solution)/shard_map/ppermute | solution.py:35
  (217 other events, 1859.3 us)
